TPU v7x, 32 devices: a whole 2x2x4 slice. The times are simulated.
32 devices in a mesh: parts: 2 (over y), gx: 4 (over z), gy: 2 (over x), gz: 2 (over core).
Axes of the slice: x: 2, y: 2, z: 4, core: 2. Of those that a mesh axis runs over, the one named last changes fastest.
Arguments:
- adjoint_source: float32 [8, 256, 1024], P(('parts', 'gz'), 'gx', 'gy'), parts along dimension 0, may hold values from -8 to 8
- node_voltage: float32 [8, 256, 1024], P(('parts', 'gz'), 'gx', 'gy'), parts along dimension 0, may hold values from -6 to 6
- class_x: int32 [8, 256, 1024], P(('parts', 'gz'), 'gx', 'gy'), parts along dimension 0, may hold values from 0 to 7
- class_y: int32 [8, 256, 1024], P(('parts', 'gz'), 'gx', 'gy'), parts along dimension 0, may hold values from 0 to 7
- via_cond: float32 [8, 256, 1024], P(('parts', 'gz'), 'gx', 'gy'), parts along dimension 0, may hold values from 0.5 to 4
- layer_sheet: float32 [4], replicated, may hold values from 0.5 to 4
- width_table: float32 [8], replicated, may hold values from 0.5 to 2
Outputs:
- adjoint: float32 [8, 256, 1024], P(('parts', 'gz'), 'gx', 'gy'), parts along dimension 0
- grad_x: float32 [8, 256, 1024], P(('parts', 'gz'), 'gx', 'gy'), parts along dimension 0
- grad_y: float32 [8, 256, 1024], P(('parts', 'gz'), 'gx', 'gy'), parts along dimension 0
- grad_via: float32 [8, 256, 1024], P(('parts', 'gz'), 'gx', 'gy'), parts along dimension 0
There are 2 independent parts, one for each index of `parts`. A program takes and returns all parts, laid end to end along the dimension named above; an argument that names none is the same for every part. Nothing has to cross between parts.
All inputs are finite; a program needn't handle non-finite values.
Results may differ from a plain program's by a relative error of at most 0.0001.
Values sent between devices are 32-bit elements; how exact they have to be, the bound alone decides.
A program may use at most 64 MiB of HBM per device.

v0:
```python
import jax
import jax.numpy as jnp
from jax import lax
from jax.sharding import PartitionSpec as P

ITERS = 2


def with_halo(shard, sides, width):
    for axis, dim in sides:
        size, length = (lax.axis_size(axis), shard.shape[dim])
        up = [(i, (i + 1) % size) for i in range(size - 1)]
        down = [(j, i) for i, j in up]
        last = lax.slice_in_dim(shard, length - width, length, axis=dim)
        leading = lax.slice_in_dim(shard, 0, width, axis=dim)
        before = lax.ppermute(last, axis, up)
        after = lax.ppermute(leading, axis, down)
        shard = jnp.concatenate([before, shard, after], axis=dim)
    return shard


def extend(stacked):
    return with_halo(stacked, (("gx", 2), ("gy", 3), ("gz", 1)), 1)


def global_sum(values):
    return lax.psum(jnp.sum(values), ("gx", "gy", "gz"))


def body(adjoint_source, node_voltage, class_x, class_y, via_cond, layer_sheet, width_table):
    lay_dev, rows_x, rows_y = adjoint_source.shape
    classes = width_table.shape[0]
    first_layer = lax.axis_index("gz") * lay_dev
    sheet = lax.dynamic_slice_in_dim(layer_sheet, first_layer, lay_dev, 0)[:, None, None]
    pos_x = lax.axis_index("gx") * rows_x + jnp.arange(rows_x, dtype=jnp.int32)
    pos_y = lax.axis_index("gy") * rows_y + jnp.arange(rows_y, dtype=jnp.int32)
    keep_x = (pos_x < rows_x * lax.axis_size("gx") - 1).astype(jnp.float32)[None, :, None]
    keep_y = (pos_y < rows_y * lax.axis_size("gy") - 1).astype(jnp.float32)[None, None, :]
    labels = jnp.arange(classes, dtype=jnp.int32)[:, None, None, None]
    table = width_table[:, None, None, None]
    width_x = jnp.sum(jnp.where(class_x[None] == labels, table, 0.0), axis=0)
    width_y = jnp.sum(jnp.where(class_y[None] == labels, table, 0.0), axis=0)
    cond_x = sheet * width_x * keep_x
    cond_y = sheet * width_y * keep_y
    edges = extend(jnp.stack([cond_x, cond_y, via_cond]))
    lower_x = edges[0, 1:-1, :-2, 1:-1]
    lower_y = edges[1, 1:-1, 1:-1, :-2]
    lower_v = edges[2, :-2, 1:-1, 1:-1]
    diagonal = cond_x + lower_x + cond_y + lower_y + via_cond + lower_v
    adjoint = jnp.zeros_like(adjoint_source)
    rim_adjoint = jnp.zeros((lay_dev + 2, rows_x + 2, rows_y + 2), jnp.float32)
    residual = adjoint_source
    precond = residual / diagonal
    direction = precond
    rho_now = global_sum(residual * precond)
    for iteration in range(ITERS):
        padded = extend(direction[None])[0]
        result = diagonal * direction
        result = result - cond_x * padded[1:-1, 2:, 1:-1] - lower_x * padded[1:-1, :-2, 1:-1]
        result = result - cond_y * padded[1:-1, 1:-1, 2:] - lower_y * padded[1:-1, 1:-1, :-2]
        result = result - via_cond * padded[2:, 1:-1, 1:-1] - lower_v * padded[:-2, 1:-1, 1:-1]
        alpha = rho_now / lax.psum(jnp.sum(direction * result), ("gx", "gy", "gz"))
        adjoint = adjoint + alpha * direction
        rim_adjoint = rim_adjoint + alpha * padded
        residual = residual - alpha * result
        precond = residual / diagonal
        rho_next = global_sum(residual * precond)
        direction = precond + rho_next / rho_now * direction
        rho_now = rho_next
    both = extend(jnp.stack([adjoint, node_voltage]))
    pad_adj = both[0]
    pad_volt = both[1]
    grad_x = (
        -sheet
        * keep_x
        * (adjoint - pad_adj[1:-1, 2:, 1:-1])
        * (node_voltage - pad_volt[1:-1, 2:, 1:-1])
    )
    grad_y = (
        -sheet
        * keep_y
        * (adjoint - pad_adj[1:-1, 1:-1, 2:])
        * (node_voltage - pad_volt[1:-1, 1:-1, 2:])
    )
    grad_via = -(adjoint - pad_adj[2:, 1:-1, 1:-1]) * (node_voltage - pad_volt[2:, 1:-1, 1:-1])
    return (adjoint, grad_x, grad_y, grad_via)


def solution(mesh):
    placed = (
        P(("parts", "gz"), "gx", "gy"),
        P(("parts", "gz"), "gx", "gy"),
        P(("parts", "gz"), "gx", "gy"),
        P(("parts", "gz"), "gx", "gy"),
        P(("parts", "gz"), "gx", "gy"),
        P(),
        P(),
    )
    return jax.shard_map(
        body,
        mesh=mesh,
        in_specs=placed,
        out_specs=(
            P(("parts", "gz"), "gx", "gy"),
            P(("parts", "gz"), "gx", "gy"),
            P(("parts", "gz"), "gx", "gy"),
            P(("parts", "gz"), "gx", "gy"),
        ),
        check_vma=False,
    )
```

profile of v0, /device:TPU:0, one launch (start us, length us, event | category | flops | bytes accessed | tf_op | source)
XLA Modules:
  0.0 191.7 jit_solution(17961793509079866448)
XLA Ops:
  1.4 1.6 select_reduce_fusion
  3.2 4.9 %collective-permute-start = (f32[3,2,1,512]{3,2,1,0:T(1,128)S(1)}, f32[3,2,1,512]{3,2,1,0:T(1,128)S(1)}, u32[]{:S(2)}, u32[]{:S(2)}) collective-permute-start(f32[3,2,1,512]{3,2,1,0:T(1,128)S(1)} %get-tuple-element.30), channel_id=1, source_target_pairs={{0,4},{4,8},{8,12},{1,5},{5,9},{9,13},{2,6},{6,10},{10,14},{3,7},{... | collective-permute-start | bytes 36872 | tf_op jit(solution)/shard_map/ppermute | solution.py:16
  9.5 4.2 %collective-permute-done.1 = f32[3,2,1,512]{3,2,1,0:T(1,128)S(1)} collective-permute-done((f32[3,2,1,512]{3,2,1,0:T(1,128)S(1)}, f32[3,2,1,512]{3,2,1,0:T(1,128)S(1)}, u32[]{:S(2)}, u32[]{:S(2)}) %collective-permute-start.1) | collective-permute-done | bytes 12320 | tf_op jit(solution)/shard_map/ppermute | solution.py:17
  13.9 3.4 %collective-permute-start.2 = (f32[3,2,66,1]{3,2,1,0:T(8,128)S(1)}, f32[3,2,66,1]{3,2,1,0:T(8,128)S(1)}, u32[]{:S(2)}, u32[]{:S(2)}) collective-permute-start(f32[3,2,66,1]{3,2,1,0:T(8,128)S(1)} %get-tuple-element.28), channel_id=1, source_target_pairs={{0,2},{1,3},{4,6},{5,7},{8,10},{9,11},{12,14},{13,15},{16,18},{17,... | collective-permute-start | bytes 4760 | tf_op jit(solution)/shard_map/ppermute | solution.py:16
  18.6 2.1 %collective-permute-done.2 = f32[3,2,66,1]{3,2,1,0:T(8,128)S(1)} collective-permute-done((f32[3,2,66,1]{3,2,1,0:T(8,128)S(1)}, f32[3,2,66,1]{3,2,1,0:T(8,128)S(1)}, u32[]{:S(2)}, u32[]{:S(2)}) %collective-permute-start.2) | collective-permute-done | bytes 1616 | tf_op jit(solution)/shard_map/ppermute | solution.py:16
  20.7 4.4 %collective-permute-done.3 = f32[3,2,66,1]{3,2,1,0:T(8,128)S(1)} collective-permute-done((f32[3,2,66,1]{3,2,1,0:T(8,128)S(1)}, f32[3,2,66,1]{3,2,1,0:T(8,128)S(1)}, u32[]{:S(2)}, u32[]{:S(2)}) %collective-permute-start.3) | collective-permute-done | bytes 1616 | tf_op jit(solution)/shard_map/ppermute | solution.py:17
  25.9 1.3 collective-permute-start.4
  27.3 1.5 collective-permute-done.4
  29.1 3.5 %collective-permute-start.5 = (f32[1,2,1,512]{3,2,1,0:T(1,128)S(1)}, f32[1,2,1,512]{3,2,1,0:T(1,128)S(1)}, u32[]{:S(2)}, u32[]{:S(2)}) collective-permute-start(f32[1,2,1,512]{3,2,1,0:T(1,128)S(1)} %get-tuple-element.47), channel_id=1, source_target_pairs={{0,4},{4,8},{8,12},{1,5},{5,9},{9,13},{2,6},{6,10},{10,14},{3,7},{... | collective-permute-start | bytes 12296 | tf_op jit(solution)/shard_map/ppermute | solution.py:16
  33.9 4.2 %collective-permute-done.6 = f32[1,2,1,512]{3,2,1,0:T(1,128)S(1)} collective-permute-done((f32[1,2,1,512]{3,2,1,0:T(1,128)S(1)}, f32[1,2,1,512]{3,2,1,0:T(1,128)S(1)}, u32[]{:S(2)}, u32[]{:S(2)}) %collective-permute-start.6) | collective-permute-done | bytes 4128 | tf_op jit(solution)/shard_map/ppermute | solution.py:17
  38.2 1.5 collective-permute-start.7
  41.6 4.3 %collective-permute-done.8 = f32[1,2,66,1]{3,2,1,0:T(8,128)S(1)} collective-permute-done((f32[1,2,66,1]{3,2,1,0:T(8,128)S(1)}, f32[1,2,66,1]{3,2,1,0:T(8,128)S(1)}, u32[]{:S(2)}, u32[]{:S(2)}) %collective-permute-start.8) | collective-permute-done | bytes 560 | tf_op jit(solution)/shard_map/ppermute | solution.py:17
  47.4 3.0 %collective-permute-start.9 = (f32[1,1,66,514]{3,2,1,0:T(8,128)S(1)}, f32[1,1,66,514]{3,2,1,0:T(8,128)S(1)}, u32[]{:S(2)}, u32[]{:S(2)}) collective-permute-start(f32[1,1,66,514]{3,2,1,0:T(8,128)S(1)} %get-tuple-element.39), channel_id=1, source_target_pairs={{0,1},{2,3},{4,5},{6,7},{8,9},{10,11},{12,13},{14,15},{16,17},{18,... | collective-permute-start | bytes 407096 | tf_op jit(solution)/shard_map/ppermute | solution.py:16
  52.8 30.5 %all-reduce = (f32[]{:T(128)}, f32[]{:T(128)}) all-reduce(f32[]{:T(128)} %get-tuple-element.9, f32[]{:T(128)} %get-tuple-element.8), channel_id=1, replica_groups=mesh['parts'=2,'gx'=4,'gy'=2,'gz'=2] {'gx','gy','gz'}, use_global_device_ids=true, to_apply=%region_3.4 | all-reduce | flops 2 | bytes 16 | tf_op jit(solution)/shard_map/psum | solution.py:27
  85.3 30.1 %psum.30 = f32[]{:T(128)} all-reduce(f32[]{:T(128)} %multiply_reduce_fusion), channel_id=1, replica_groups=mesh['parts'=2,'gx'=4,'gy'=2,'gz'=2] {'gx','gy','gz'}, use_global_device_ids=true, to_apply=%region_7.8 | all-reduce | flops 1 | bytes 8 | tf_op jit(solution)/shard_map/psum | solution.py:27
  119.5 4.2 %collective-permute-done.12 = f32[1,2,1,512]{3,2,1,0:T(1,128)S(1)} collective-permute-done((f32[1,2,1,512]{3,2,1,0:T(1,128)S(1)}, f32[1,2,1,512]{3,2,1,0:T(1,128)S(1)}, u32[]{:S(2)}, u32[]{:S(2)}) %collective-permute-start.12) | collective-permute-done | bytes 4128 | tf_op jit(solution)/shard_map/ppermute | solution.py:17
  127.0 4.3 %collective-permute-done.14 = f32[1,2,66,1]{3,2,1,0:T(8,128)S(1)} collective-permute-done((f32[1,2,66,1]{3,2,1,0:T(8,128)S(1)}, f32[1,2,66,1]{3,2,1,0:T(8,128)S(1)}, u32[]{:S(2)}, u32[]{:S(2)}) %collective-permute-start.14) | collective-permute-done | bytes 560 | tf_op jit(solution)/shard_map/ppermute | solution.py:17
  134.2 2.0 %collective-permute-done.16 = f32[1,1,66,514]{3,2,1,0:T(8,128)S(1)} collective-permute-done((f32[1,1,66,514]{3,2,1,0:T(8,128)S(1)}, f32[1,1,66,514]{3,2,1,0:T(8,128)S(1)}, u32[]{:S(2)}, u32[]{:S(2)}) %collective-permute-start.16) | collective-permute-done | bytes 135728 | tf_op jit(solution)/shard_map/ppermute | solution.py:17
  137.5 30.2 %psum.31 = f32[]{:T(128)} all-reduce(f32[]{:T(128)} %fusion.16), channel_id=1, replica_groups=mesh['parts'=2,'gx'=4,'gy'=2,'gz'=2] {'gx','gy','gz'}, use_global_device_ids=true, to_apply=%region_9.10 | all-reduce | flops 1 | bytes 8 | tf_op jit(solution)/shard_map/psum | solution.py:62
  171.8 4.2 %collective-permute-done.18 = f32[2,2,1,512]{3,2,1,0:T(1,128)S(1)} collective-permute-done((f32[2,2,1,512]{3,2,1,0:T(1,128)S(1)}, f32[2,2,1,512]{3,2,1,0:T(1,128)S(1)}, u32[]{:S(2)}, u32[]{:S(2)}) %collective-permute-start.18) | collective-permute-done | bytes 8224 | tf_op jit(solution)/shard_map/ppermute | solution.py:17
  178.7 1.3 collective-permute-done.19
  180.1 4.4 %collective-permute-done.20 = f32[2,2,66,1]{3,2,1,0:T(8,128)S(1)} collective-permute-done((f32[2,2,66,1]{3,2,1,0:T(8,128)S(1)}, f32[2,2,66,1]{3,2,1,0:T(8,128)S(1)}, u32[]{:S(2)}, u32[]{:S(2)}) %collective-permute-start.20) | collective-permute-done | bytes 1088 | tf_op jit(solution)/shard_map/ppermute | solution.py:17
  187.6 2.1 %collective-permute-done.22 = f32[2,1,66,514]{3,2,1,0:T(8,128)S(1)} collective-permute-done((f32[2,1,66,514]{3,2,1,0:T(8,128)S(1)}, f32[2,1,66,514]{3,2,1,0:T(8,128)S(1)}, u32[]{:S(2)}, u32[]{:S(2)}) %collective-permute-start.22) | collective-permute-done | bytes 271424 | tf_op jit(solution)/shard_map/ppermute | solution.py:17
  190.3 1.4 fusion.8
  (68 shorter events, 31.9 us)
Async XLA Ops:
  3.2 6.3 %collective-permute-start = (f32[3,2,1,512]{3,2,1,0:T(1,128)S(1)}, f32[3,2,1,512]{3,2,1,0:T(1,128)S(1)}, u32[]{:S(2)}, u32[]{:S(2)}) collective-permute-start(f32[3,2,1,512]{3,2,1,0:T(1,128)S(1)} %get-tuple-element.30), channel_id=1, source_target_pairs={{0,4},{4,8},{8,12},{1,5},{5,9},{9,13},{2,6},{6,10},{10,14},{3,7},{... | collective-permute-start | bytes 36872 | tf_op jit(solution)/shard_map/ppermute | solution.py:16
  8.1 5.6 %collective-permute-start.1 = (f32[3,2,1,512]{3,2,1,0:T(1,128)S(1)}, f32[3,2,1,512]{3,2,1,0:T(1,128)S(1)}, u32[]{:S(2)}, u32[]{:S(2)}) collective-permute-start(f32[3,2,1,512]{3,2,1,0:T(1,128)S(1)} %get-tuple-element.29), channel_id=1, source_target_pairs={{4,0},{8,4},{12,8},{5,1},{9,5},{13,9},{6,2},{10,6},{14,10},{7,3},{... | collective-permute-start | bytes 36872 | tf_op jit(solution)/shard_map/ppermute | solution.py:17
  13.9 6.8 %collective-permute-start.2 = (f32[3,2,66,1]{3,2,1,0:T(8,128)S(1)}, f32[3,2,66,1]{3,2,1,0:T(8,128)S(1)}, u32[]{:S(2)}, u32[]{:S(2)}) collective-permute-start(f32[3,2,66,1]{3,2,1,0:T(8,128)S(1)} %get-tuple-element.28), channel_id=1, source_target_pairs={{0,2},{1,3},{4,6},{5,7},{8,10},{9,11},{12,14},{13,15},{16,18},{17,... | collective-permute-start | bytes 4760 | tf_op jit(solution)/shard_map/ppermute | solution.py:16
  17.3 7.8 %collective-permute-start.3 = (f32[3,2,66,1]{3,2,1,0:T(8,128)S(1)}, f32[3,2,66,1]{3,2,1,0:T(8,128)S(1)}, u32[]{:S(2)}, u32[]{:S(2)}) collective-permute-start(f32[3,2,66,1]{3,2,1,0:T(8,128)S(1)} %get-tuple-element.27), channel_id=1, source_target_pairs={{2,0},{3,1},{6,4},{7,5},{10,8},{11,9},{14,12},{15,13},{18,16},{19,... | collective-permute-start | bytes 4760 | tf_op jit(solution)/shard_map/ppermute | solution.py:17
  25.9 2.8 %collective-permute-start.4 = (f32[3,1,66,514]{3,1,2,0:T(1,128)S(1)}, f32[3,1,66,514]{3,1,2,0:T(1,128)S(1)}, u32[]{:S(2)}, u32[]{:S(2)}) collective-permute-start(f32[3,1,66,514]{3,1,2,0:T(1,128)S(1)} %copy.26), channel_id=1, source_target_pairs={{0,1},{2,3},{4,5},{6,7},{8,9},{10,11},{12,13},{14,15},{16,17},{18,... | collective-permute-start | bytes 1221272 | tf_op jit(solution)/shard_map/ppermute | solution.py:16
  29.1 4.8 %collective-permute-start.5 = (f32[1,2,1,512]{3,2,1,0:T(1,128)S(1)}, f32[1,2,1,512]{3,2,1,0:T(1,128)S(1)}, u32[]{:S(2)}, u32[]{:S(2)}) collective-permute-start(f32[1,2,1,512]{3,2,1,0:T(1,128)S(1)} %get-tuple-element.47), channel_id=1, source_target_pairs={{0,4},{4,8},{8,12},{1,5},{5,9},{9,13},{2,6},{6,10},{10,14},{3,7},{... | collective-permute-start | bytes 12296 | tf_op jit(solution)/shard_map/ppermute | solution.py:16
  32.6 5.5 %collective-permute-start.6 = (f32[1,2,1,512]{3,2,1,0:T(1,128)S(1)}, f32[1,2,1,512]{3,2,1,0:T(1,128)S(1)}, u32[]{:S(2)}, u32[]{:S(2)}) collective-permute-start(f32[1,2,1,512]{3,2,1,0:T(1,128)S(1)} %get-tuple-element.48), channel_id=1, source_target_pairs={{4,0},{8,4},{12,8},{5,1},{9,5},{13,9},{6,2},{10,6},{14,10},{7,3},{... | collective-permute-start | bytes 12296 | tf_op jit(solution)/shard_map/ppermute | solution.py:17
  38.2 3.4 %collective-permute-start.7 = (f32[1,2,66,1]{3,2,1,0:T(8,128)S(1)}, f32[1,2,66,1]{3,2,1,0:T(8,128)S(1)}, u32[]{:S(2)}, u32[]{:S(2)}) collective-permute-start(f32[1,2,66,1]{3,2,1,0:T(8,128)S(1)} %get-tuple-element.43), channel_id=1, source_target_pairs={{0,2},{1,3},{4,6},{5,7},{8,10},{9,11},{12,14},{13,15},{16,18},{17,... | collective-permute-start | bytes 1592 | tf_op jit(solution)/shard_map/ppermute | solution.py:16
  39.6 6.2 %collective-permute-start.8 = (f32[1,2,66,1]{3,2,1,0:T(8,128)S(1)}, f32[1,2,66,1]{3,2,1,0:T(8,128)S(1)}, u32[]{:S(2)}, u32[]{:S(2)}) collective-permute-start(f32[1,2,66,1]{3,2,1,0:T(8,128)S(1)} %get-tuple-element.44), channel_id=1, source_target_pairs={{2,0},{3,1},{6,4},{7,5},{10,8},{11,9},{14,12},{15,13},{18,16},{19,... | collective-permute-start | bytes 1592 | tf_op jit(solution)/shard_map/ppermute | solution.py:17
  46.1 4.4 %collective-permute-start.10 = (f32[1,1,66,514]{3,2,1,0:T(8,128)S(1)}, f32[1,1,66,514]{3,2,1,0:T(8,128)S(1)}, u32[]{:S(2)}, u32[]{:S(2)}) collective-permute-start(f32[1,1,66,514]{3,2,1,0:T(8,128)S(1)} %get-tuple-element.40), channel_id=1, source_target_pairs={{1,0},{3,2},{5,4},{7,6},{9,8},{11,10},{13,12},{15,14},{17,16},{19,... | collective-permute-start | bytes 407096 | tf_op jit(solution)/shard_map/ppermute | solution.py:17
  47.4 4.1 %collective-permute-start.9 = (f32[1,1,66,514]{3,2,1,0:T(8,128)S(1)}, f32[1,1,66,514]{3,2,1,0:T(8,128)S(1)}, u32[]{:S(2)}, u32[]{:S(2)}) collective-permute-start(f32[1,1,66,514]{3,2,1,0:T(8,128)S(1)} %get-tuple-element.39), channel_id=1, source_target_pairs={{0,1},{2,3},{4,5},{6,7},{8,9},{10,11},{12,13},{14,15},{16,17},{18,... | collective-permute-start | bytes 407096 | tf_op jit(solution)/shard_map/ppermute | solution.py:16
  116.9 2.6 %collective-permute-start.11 = (f32[1,2,1,512]{3,2,1,0:T(1,128)S(1)}, f32[1,2,1,512]{3,2,1,0:T(1,128)S(1)}, u32[]{:S(2)}, u32[]{:S(2)}) collective-permute-start(f32[1,2,1,512]{3,2,1,0:T(1,128)S(1)} %get-tuple-element.45), channel_id=1, source_target_pairs={{0,4},{4,8},{8,12},{1,5},{5,9},{9,13},{2,6},{6,10},{10,14},{3,7},{... | collective-permute-start | bytes 12296 | tf_op jit(solution)/shard_map/ppermute | solution.py:16
  118.2 5.5 %collective-permute-start.12 = (f32[1,2,1,512]{3,2,1,0:T(1,128)S(1)}, f32[1,2,1,512]{3,2,1,0:T(1,128)S(1)}, u32[]{:S(2)}, u32[]{:S(2)}) collective-permute-start(f32[1,2,1,512]{3,2,1,0:T(1,128)S(1)} %get-tuple-element.46), channel_id=1, source_target_pairs={{4,0},{8,4},{12,8},{5,1},{9,5},{13,9},{6,2},{10,6},{14,10},{7,3},{... | collective-permute-start | bytes 12296 | tf_op jit(solution)/shard_map/ppermute | solution.py:17
  123.8 3.3 %collective-permute-start.13 = (f32[1,2,66,1]{3,2,1,0:T(8,128)S(1)}, f32[1,2,66,1]{3,2,1,0:T(8,128)S(1)}, u32[]{:S(2)}, u32[]{:S(2)}) collective-permute-start(f32[1,2,66,1]{3,2,1,0:T(8,128)S(1)} %get-tuple-element.41), channel_id=1, source_target_pairs={{0,2},{1,3},{4,6},{5,7},{8,10},{9,11},{12,14},{13,15},{16,18},{17,... | collective-permute-start | bytes 1592 | tf_op jit(solution)/shard_map/ppermute | solution.py:16
  125.1 6.2 %collective-permute-start.14 = (f32[1,2,66,1]{3,2,1,0:T(8,128)S(1)}, f32[1,2,66,1]{3,2,1,0:T(8,128)S(1)}, u32[]{:S(2)}, u32[]{:S(2)}) collective-permute-start(f32[1,2,66,1]{3,2,1,0:T(8,128)S(1)} %get-tuple-element.42), channel_id=1, source_target_pairs={{2,0},{3,1},{6,4},{7,5},{10,8},{11,9},{14,12},{15,13},{18,16},{19,... | collective-permute-start | bytes 1592 | tf_op jit(solution)/shard_map/ppermute | solution.py:17
  131.5 2.6 %collective-permute-start.15 = (f32[1,1,66,514]{3,2,1,0:T(8,128)S(1)}, f32[1,1,66,514]{3,2,1,0:T(8,128)S(1)}, u32[]{:S(2)}, u32[]{:S(2)}) collective-permute-start(f32[1,1,66,514]{3,2,1,0:T(8,128)S(1)} %get-tuple-element.37), channel_id=1, source_target_pairs={{0,1},{2,3},{4,5},{6,7},{8,9},{10,11},{12,13},{14,15},{16,17},{18,... | collective-permute-start | bytes 407096 | tf_op jit(solution)/shard_map/ppermute | solution.py:16
  132.9 3.3 %collective-permute-start.16 = (f32[1,1,66,514]{3,2,1,0:T(8,128)S(1)}, f32[1,1,66,514]{3,2,1,0:T(8,128)S(1)}, u32[]{:S(2)}, u32[]{:S(2)}) collective-permute-start(f32[1,1,66,514]{3,2,1,0:T(8,128)S(1)} %get-tuple-element.38), channel_id=1, source_target_pairs={{1,0},{3,2},{5,4},{7,6},{9,8},{11,10},{13,12},{15,14},{17,16},{19,... | collective-permute-start | bytes 407096 | tf_op jit(solution)/shard_map/ppermute | solution.py:17
  136.4 32.7 %copy-start.2 = (f32[2,64,512]{2,1,0:T(8,128)S(1)}, f32[2,64,512]{2,1,0:T(8,128)}, u32[]{:S(2)}) copy-start(f32[2,64,512]{2,1,0:T(8,128)} %param.8) | copy-start | bytes 786436
  169.2 2.6 %collective-permute-start.17 = (f32[2,2,1,512]{3,2,1,0:T(1,128)S(1)}, f32[2,2,1,512]{3,2,1,0:T(1,128)S(1)}, u32[]{:S(2)}, u32[]{:S(2)}) collective-permute-start(f32[2,2,1,512]{3,2,1,0:T(1,128)S(1)} %get-tuple-element.35), channel_id=1, source_target_pairs={{0,4},{4,8},{8,12},{1,5},{5,9},{9,13},{2,6},{6,10},{10,14},{3,7},{... | collective-permute-start | bytes 24584 | tf_op jit(solution)/shard_map/ppermute | solution.py:16
  170.5 5.5 %collective-permute-start.18 = (f32[2,2,1,512]{3,2,1,0:T(1,128)S(1)}, f32[2,2,1,512]{3,2,1,0:T(1,128)S(1)}, u32[]{:S(2)}, u32[]{:S(2)}) collective-permute-start(f32[2,2,1,512]{3,2,1,0:T(1,128)S(1)} %get-tuple-element.36), channel_id=1, source_target_pairs={{4,0},{8,4},{12,8},{5,1},{9,5},{13,9},{6,2},{10,6},{14,10},{7,3},{... | collective-permute-start | bytes 24584 | tf_op jit(solution)/shard_map/ppermute | solution.py:17
  176.1 4.0 %collective-permute-start.19 = (f32[2,2,66,1]{3,2,1,0:T(8,128)S(1)}, f32[2,2,66,1]{3,2,1,0:T(8,128)S(1)}, u32[]{:S(2)}, u32[]{:S(2)}) collective-permute-start(f32[2,2,66,1]{3,2,1,0:T(8,128)S(1)} %get-tuple-element.33), channel_id=1, source_target_pairs={{0,2},{1,3},{4,6},{5,7},{8,10},{9,11},{12,14},{13,15},{16,18},{17,... | collective-permute-start | bytes 3176 | tf_op jit(solution)/shard_map/ppermute | solution.py:16
  177.4 7.0 %collective-permute-start.20 = (f32[2,2,66,1]{3,2,1,0:T(8,128)S(1)}, f32[2,2,66,1]{3,2,1,0:T(8,128)S(1)}, u32[]{:S(2)}, u32[]{:S(2)}) collective-permute-start(f32[2,2,66,1]{3,2,1,0:T(8,128)S(1)} %get-tuple-element.34), channel_id=1, source_target_pairs={{2,0},{3,1},{6,4},{7,5},{10,8},{11,9},{14,12},{15,13},{18,16},{19,... | collective-permute-start | bytes 3176 | tf_op jit(solution)/shard_map/ppermute | solution.py:17
  184.9 2.8 %collective-permute-start.21 = (f32[2,1,66,514]{3,2,1,0:T(8,128)S(1)}, f32[2,1,66,514]{3,2,1,0:T(8,128)S(1)}, u32[]{:S(2)}, u32[]{:S(2)}) collective-permute-start(f32[2,1,66,514]{3,2,1,0:T(8,128)S(1)} %get-tuple-element.31), channel_id=1, source_target_pairs={{0,1},{2,3},{4,5},{6,7},{8,9},{10,11},{12,13},{14,15},{16,17},{18,... | collective-permute-start | bytes 814184 | tf_op jit(solution)/shard_map/ppermute | solution.py:16
  186.2 3.6 %collective-permute-start.22 = (f32[2,1,66,514]{3,2,1,0:T(8,128)S(1)}, f32[2,1,66,514]{3,2,1,0:T(8,128)S(1)}, u32[]{:S(2)}, u32[]{:S(2)}) collective-permute-start(f32[2,1,66,514]{3,2,1,0:T(8,128)S(1)} %get-tuple-element.32), channel_id=1, source_target_pairs={{1,0},{3,2},{5,4},{7,6},{9,8},{11,10},{13,12},{15,14},{17,16},{19,... | collective-permute-start | bytes 814184 | tf_op jit(solution)/shard_map/ppermute | solution.py:17
  (3 other events, 27.0 us)
where the time goes:
time: 192 us
  blocking collectives  90.8 us (47%)
  waiting for transfers between devices  45.7 us (24%)
  starting transfers between devices  39.7 us (21%)
  other arithmetic  9.56 us (5%)
  between operations  5.13 us (3%)
    psum x2, blocking collectives, global_sum(): return lax.psum(jnp.sum(values), ('gx', 'gy', 'gz'))  60.6 us
    ppermute x11, waiting for transfers between devices, with_halo(): after = lax.ppermute(leading, axis, down)  38.3 us
    psum x1, blocking collectives, body(): alpha = rho_now / lax.psum(jnp.sum(direction * result), ('gx', 'gy', 'gz'))  30.2 us
    ppermute x12, starting transfers between devices, with_halo(): before = lax.ppermute(last, axis, up)  25.4 us
    ppermute x11, starting transfers between devices, with_halo(): after = lax.ppermute(leading, axis, down)  14.2 us
    ppermute x12, waiting for transfers between devices, with_halo(): before = lax.ppermute(last, axis, up)  7.43 us
  transfers between devices with their start and end apart: 23, of which 17 were waited for; matrix products, arithmetic and copies ran while one was open for 0% of the time, Pallas kernels for 0%

commit v1 on v0

v1 whole, which is shorter than its diff:
```python
import functools

import jax
import jax.numpy as jnp
from jax import lax
from jax.experimental import pallas as pl
from jax.experimental.pallas import tpu as pltpu
from jax.sharding import PartitionSpec as P

F32 = jnp.float32
PAD = 8
ROWS = 16
LANES = 128
MESSAGES = {
    "cx": ("gx", 1), "cy": ("gy", 1), "cv": ("gz", 1),
    "vx": ("gx", -1), "vy": ("gy", -1), "vl": ("gz", -1),
    "zx_up": ("gx", 1), "zx_dn": ("gx", -1),
    "zy_up": ("gy", 1), "zy_dn": ("gy", -1),
    "zl_up": ("gz", 1), "zl_dn": ("gz", -1),
    "tx": ("gx", -1), "ty": ("gy", -1), "tl": ("gz", -1),
}
NAMES = list(MESSAGES)


def kernel(
    sizes, dims,
    source_hbm, volt_hbm, class_x_hbm, class_y_hbm, via_hbm, sheet_ref, table_ref,
    adj_ref, grad_x_ref, grad_y_ref, grad_v_ref,
    source, volt, class_x, class_y, via, cond_x, cond_y, low_y, inverse, z, t, adj,
    row_send, row_recv, col_send, col_recv, lay_recv, part, parts,
    load_sem, send_sem, recv_sem, part_send, part_recv,
):
    lay, nx, ny = dims
    group = sizes["gx"] * sizes["gy"] * sizes["gz"]
    here = {axis: lax.axis_index(axis) for axis in ("gx", "gy", "gz")}
    me = (here["gx"] * sizes["gy"] + here["gy"]) * sizes["gz"] + here["gz"]
    inner = pl.ds(PAD, nx)
    first, last = PAD, PAD + nx - 1

    loads = []
    for i, (src, dst) in enumerate((
        (class_x_hbm, class_x), (class_y_hbm, class_y), (via_hbm, via),
        (source_hbm, source), (volt_hbm, volt.at[:, inner, :]),
    )):
        copy = pltpu.make_async_copy(src, dst, load_sem.at[i])
        copy.start()
        loads.append(copy)

    row_recv[...] = jnp.zeros_like(row_recv)
    col_recv[...] = jnp.zeros_like(col_recv)
    lay_recv[...] = jnp.zeros_like(lay_recv)

    def place(rank):
        gz = lax.rem(rank, sizes["gz"])
        rest = lax.div(rank, sizes["gz"])
        return {"gx": lax.div(rest, sizes["gy"]), "gy": lax.rem(rest, sizes["gy"]), "gz": gz}

    barrier = pltpu.get_barrier_semaphore()

    def each_peer(body):
        if group <= 32:
            for k in range(1, group):
                body(lax.rem(me + k, group))
        else:
            lax.fori_loop(1, group, lambda k, c: (body(lax.rem(me + k, group)), c)[1], 0)

    each_peer(lambda peer: pl.semaphore_signal(
        barrier, inc=1, device_id=place(peer), device_id_type=pl.DeviceIdType.MESH))

    ROW = {"cx": 0, "vx": 1, "zx_up": 2, "zx_dn": 3, "tx": 4}
    COL = {"cy": 0, "vy": 1, "zy_up": 2, "zy_dn": 3, "ty": 4}
    LAY = {"cv": 0, "vl": 1, "zl_up": 2, "zl_dn": 3, "tl": 4}
    LAY_SRC = {
        "cv": via.at[lay - 1], "vl": volt.at[0, inner, :], "zl_up": z.at[lay - 1, inner, :],
        "zl_dn": z.at[0, inner, :], "tl": t.at[0, inner, :],
    }

    def message(name):
        axis, way = MESSAGES[name]
        i = NAMES.index(name)
        if name in ROW:
            src, dst = row_send.at[ROW[name]], row_recv.at[ROW[name]]
        elif name in COL:
            src, dst = col_send.at[COL[name]], col_recv.at[COL[name]]
        else:
            src, dst = LAY_SRC[name], lay_recv.at[LAY[name]]
        size = sizes[axis]
        to = lax.rem(here[axis] + (way + size), size)
        return pltpu.make_async_remote_copy(
            src_ref=src, dst_ref=dst, send_sem=send_sem.at[i], recv_sem=recv_sem.at[i],
            device_id={axis: to}, device_id_type=pl.DeviceIdType.MESH)

    def at_end(axis, way):
        return here[axis] == (sizes[axis] - 1 if way > 0 else 0)

    def send(*names):
        for name in names:
            axis, way = MESSAGES[name]
            if sizes[axis] > 1:
                pl.when(jnp.logical_not(at_end(axis, way)))(message(name).start)

    def receive(*names):
        for name in names:
            axis, way = MESSAGES[name]
            if sizes[axis] > 1:
                pl.when(jnp.logical_not(at_end(axis, -way)))(message(name).wait_recv)

    def sent(*names):
        for name in names:
            axis, way = MESSAGES[name]
            if sizes[axis] > 1:
                pl.when(jnp.logical_not(at_end(axis, way)))(message(name).wait_send)

    chunks = [(l, r) for l in range(lay) for r in range(0, nx, ROWS)]
    lane = lax.broadcasted_iota(jnp.int32, (ROWS, LANES), 1)

    def put_col(name, tile, at):
        col_send[COL[name]] = tile.reshape(lay * nx, LANES).T[at:at + 1, :]

    def col_halo(name):
        row = col_recv[COL[name]]
        return jnp.broadcast_to(row, (LANES, lay * nx)).T

    def from_left(value, edge):
        moved = pltpu.roll(value, 1, 1)
        head = jnp.where(lane == 0, edge, moved[:, :LANES])
        return jnp.concatenate([head, moved[:, LANES:]], axis=1)

    def from_right(value, edge):
        moved = pltpu.roll(value, ny - 1, 1)
        tail = jnp.where(lane == LANES - 1, edge, moved[:, ny - LANES:])
        return jnp.concatenate([moved[:, :ny - LANES], tail], axis=1)

    def edge_of(halo, l, r):
        return halo[l * nx + r:l * nx + r + ROWS]

    sheets = [sheet_ref[here["gz"] * lay + l] for l in range(lay)]
    classes = table_ref.shape[0]

    def look_up(label, l):
        value = jnp.full(label.shape, sheets[l] * table_ref[classes - 1], F32)
        for c in range(classes - 1):
            value = jnp.where(label == c, sheets[l] * table_ref[c], value)
        return value

    loads[0].wait()
    for l, r in chunks:
        cond_x[l, PAD + r:PAD + r + ROWS, :] = look_up(class_x[l, r:r + ROWS, :], l)

    @pl.when(at_end("gx", 1))
    def _():
        cond_x[:, last, :] = jnp.zeros((lay, ny), F32)

    loads[1].wait()
    for l, r in chunks:
        cond_y[l, r:r + ROWS, :] = look_up(class_y[l, r:r + ROWS, :], l)

    @pl.when(at_end("gy", 1))
    def _():
        for l in range(lay):
            tile = cond_y[l, :, ny - LANES:]
            spot = lax.broadcasted_iota(jnp.int32, tile.shape, 1)
            cond_y[l, :, ny - LANES:] = jnp.where(spot == LANES - 1, 0.0, tile)

    row_send[ROW["cx"]] = cond_x[:, last, :]
    put_col("cy", cond_y[:, :, ny - LANES:], LANES - 1)
    loads[2].wait()
    loads[3].wait()
    loads[4].wait()
    row_send[ROW["vx"]] = volt[:, first, :]
    put_col("vy", volt[:, inner, :LANES], 0)
    pl.semaphore_wait(barrier, group - 1)
    send("cv", "cx", "cy", "vx", "vy", "vl")
    receive("cx", "cy", "cv")

    cond_x[:, PAD - 1, :] = row_recv[ROW["cx"]]
    halo = col_halo("cy")
    moment0 = jnp.zeros((ROWS, ny), F32)
    for l, r in chunks:
        rows = slice(r, r + ROWS)
        cy = cond_y[l, rows, :]
        ly = from_left(cy, edge_of(halo, l, r))
        low_y[l, rows, :] = ly
        below = via[l - 1, rows, :] if l > 0 else lay_recv[LAY["cv"], rows, :]
        total = (cond_x[l, PAD + r:PAD + r + ROWS, :] + cond_x[l, PAD - 1 + r:PAD - 1 + r + ROWS, :]
                 + cy + ly + via[l, rows, :] + below)
        inv = 1.0 / total
        inverse[l, rows, :] = inv
        value = source[l, rows, :] * inv
        z[l, PAD + r:PAD + r + ROWS, :] = value
        moment0 = moment0 + source[l, rows, :] * value
    row_send[ROW["zx_up"]] = z[:, last, :]
    row_send[ROW["zx_dn"]] = z[:, first, :]
    put_col("zy_up", z[:, inner, ny - LANES:], LANES - 1)
    put_col("zy_dn", z[:, inner, :LANES], 0)
    send("zl_up", "zl_dn", "zx_up", "zx_dn", "zy_up", "zy_dn")

    receive("vx", "vy", "vl")
    volt[:, last + 1, :] = row_recv[ROW["vx"]]
    halo = col_halo("vy")
    for l, r in chunks:
        rows = slice(r, r + ROWS)
        v = volt[l, PAD + r:PAD + r + ROWS, :]
        above = volt[l + 1, PAD + r:PAD + r + ROWS, :] if l + 1 < lay else lay_recv[LAY["vl"], rows, :]
        grad_x_ref[l, rows, :] = -sheets[l] * (v - volt[l, PAD + 1 + r:PAD + 1 + r + ROWS, :])
        grad_y_ref[l, rows, :] = -sheets[l] * (v - from_right(v, edge_of(halo, l, r)))
        grad_v_ref[l, rows, :] = above - v

    @pl.when(at_end("gx", 1))
    def _():
        grad_x_ref[:, nx - 1, :] = jnp.zeros((lay, ny), F32)

    @pl.when(at_end("gy", 1))
    def _():
        for l in range(lay):
            tile = grad_y_ref[l, :, ny - LANES:]
            spot = lax.broadcasted_iota(jnp.int32, tile.shape, 1)
            grad_y_ref[l, :, ny - LANES:] = jnp.where(spot == LANES - 1, 0.0, tile)

    receive("zx_up", "zx_dn", "zy_up", "zy_dn", "zl_up", "zl_dn")
    z[:, PAD - 1, :] = row_recv[ROW["zx_up"]]
    z[:, last + 1, :] = row_recv[ROW["zx_dn"]]
    halo_lo = col_halo("zy_up")
    halo_hi = col_halo("zy_dn")
    moment1 = jnp.zeros((ROWS, ny), F32)
    moment2 = jnp.zeros((ROWS, ny), F32)
    for l, r in chunks:
        rows = slice(r, r + ROWS)
        mid = slice(PAD + r, PAD + r + ROWS)
        lower = slice(PAD - 1 + r, PAD - 1 + r + ROWS)
        upper = slice(PAD + 1 + r, PAD + 1 + r + ROWS)
        here_z = z[l, mid, :]
        z_above = z[l + 1, mid, :] if l + 1 < lay else lay_recv[LAY["zl_dn"], rows, :]
        z_below = z[l - 1, mid, :] if l > 0 else lay_recv[LAY["zl_up"], rows, :]
        below = via[l - 1, rows, :] if l > 0 else lay_recv[LAY["cv"], rows, :]
        s = cond_x[l, mid, :] * z[l, upper, :] + cond_x[l, lower, :] * z[l, lower, :]
        s = s + cond_y[l, rows, :] * from_right(here_z, edge_of(halo_hi, l, r))
        s = s + low_y[l, rows, :] * from_left(here_z, edge_of(halo_lo, l, r))
        s = s + via[l, rows, :] * z_above + below * z_below
        value = s * inverse[l, rows, :]
        t[l, mid, :] = value
        moment1 = moment1 + here_z * s
        moment2 = moment2 + value * s
    row_send[ROW["tx"]] = t[:, first, :]
    put_col("ty", t[:, inner, :LANES], 0)
    send("tl", "tx", "ty")
    receive("tx", "ty", "tl")
    t[:, last + 1, :] = row_recv[ROW["tx"]]
    halo_t = col_halo("ty")
    moment3 = jnp.zeros((ROWS, ny), F32)
    for l, r in chunks:
        rows = slice(r, r + ROWS)
        mid = slice(PAD + r, PAD + r + ROWS)
        upper = slice(PAD + 1 + r, PAD + 1 + r + ROWS)
        here_t = t[l, mid, :]
        t_above = t[l + 1, mid, :] if l + 1 < lay else lay_recv[LAY["tl"], rows, :]
        s = cond_x[l, mid, :] * t[l, upper, :]
        s = s + cond_y[l, rows, :] * from_right(here_t, edge_of(halo_t, l, r))
        s = s + via[l, rows, :] * t_above
        moment3 = moment3 + here_t * s

    def fold(value):
        wide = sum(value[:, k:k + LANES] for k in range(0, ny, LANES))
        return jnp.sum(wide, axis=0, keepdims=True)

    part[0:1, :] = fold(moment0)
    part[1:2, :] = fold(moment1)
    part[2:3, :] = fold(moment2)
    part[3:4, :] = 2.0 * fold(moment3)
    part[4:8, :] = jnp.zeros((4, LANES), F32)

    def share(peer, slot):
        return pltpu.make_async_remote_copy(
            src_ref=part, dst_ref=parts.at[slot], send_sem=part_send.at[peer], recv_sem=part_recv.at[slot],
            device_id=place(peer), device_id_type=pl.DeviceIdType.MESH)

    each_peer(lambda peer: share(peer, me).start())
    parts[me] = part[...]
    each_peer(lambda peer: share(peer, peer).wait_recv())
    totals = jnp.sum(jnp.sum(parts[...], axis=0), axis=1, keepdims=True)
    c0, c1, c2, c3 = (totals[k:k + 1, :] for k in range(4))
    curve = c0 - c1
    alpha = c0 / curve
    rest = -c1 / curve
    rho = rest * rest * c0 + 2.0 * rest * alpha * c1 + alpha * alpha * c2
    beta = rho / c0
    cross = rest * curve + alpha * (c1 - c2)
    own = rest * rest * curve + 2.0 * rest * alpha * (c1 - c2) + alpha * alpha * (c2 - c3)
    alpha_next = rho / (own + 2.0 * beta * cross + beta * beta * curve)
    factor_z = jnp.broadcast_to(alpha + alpha_next * (rest + beta), (1, ny))
    factor_t = jnp.broadcast_to(alpha_next * alpha, (1, ny))

    adj[:, last + 1, :] = factor_z * z[:, last + 1, :] + factor_t * t[:, last + 1, :]
    for l, r in chunks:
        mid = slice(PAD + r, PAD + r + ROWS)
        value = factor_z * z[l, mid, :] + factor_t * t[l, mid, :]
        adj[l, mid, :] = value
        adj_ref[l, r:r + ROWS, :] = value
    halo = factor_z[:, :LANES] * halo_hi + factor_t[:, :LANES] * halo_t
    for l, r in chunks:
        rows = slice(r, r + ROWS)
        mid = slice(PAD + r, PAD + r + ROWS)
        upper = slice(PAD + 1 + r, PAD + 1 + r + ROWS)
        value = adj[l, mid, :]
        if l + 1 < lay:
            above = adj[l + 1, mid, :]
        else:
            above = factor_z * lay_recv[LAY["zl_dn"], rows, :] + factor_t * lay_recv[LAY["tl"], rows, :]
        grad_x_ref[l, rows, :] = grad_x_ref[l, rows, :] * (value - adj[l, upper, :])
        grad_y_ref[l, rows, :] = grad_y_ref[l, rows, :] * (value - from_right(value, edge_of(halo, l, r)))
        grad_v_ref[l, rows, :] = grad_v_ref[l, rows, :] * (value - above)

    sent(*NAMES)
    each_peer(lambda peer: share(peer, me).wait_send())


def body(sizes, *args):
    lay, nx, ny = args[0].shape
    group = sizes["gx"] * sizes["gy"] * sizes["gz"]
    block = jax.ShapeDtypeStruct((lay, nx, ny), F32)
    whole = pl.BlockSpec(memory_space=pl.ANY)
    scalars = pl.BlockSpec(memory_space=pltpu.SMEM)
    vmem = pl.BlockSpec(memory_space=pltpu.VMEM)
    flat = lambda dtype=F32: pltpu.VMEM((lay, nx, ny), dtype)
    tall = pltpu.VMEM((lay, nx + 2 * PAD, ny), F32)
    return pl.pallas_call(
        functools.partial(kernel, sizes, (lay, nx, ny)),
        out_shape=(block,) * 4,
        in_specs=[whole] * 5 + [scalars] * 2,
        out_specs=(vmem,) * 4,
        scratch_shapes=[
            flat(), tall, flat(jnp.int32), flat(jnp.int32), flat(),
            tall, flat(), flat(), flat(), tall, tall, tall,
            pltpu.VMEM((5, lay, ny), F32), pltpu.VMEM((5, lay, ny), F32),
            pltpu.VMEM((5, 1, lay * nx), F32), pltpu.VMEM((5, 1, lay * nx), F32),
            pltpu.VMEM((5, nx, ny), F32),
            pltpu.VMEM((8, LANES), F32), pltpu.VMEM((group, 8, LANES), F32),
            pltpu.SemaphoreType.DMA((5,)),
            pltpu.SemaphoreType.DMA((len(NAMES),)), pltpu.SemaphoreType.DMA((len(NAMES),)),
            pltpu.SemaphoreType.DMA((group,)), pltpu.SemaphoreType.DMA((group,)),
        ],
        compiler_params=pltpu.CompilerParams(
            collective_id=0, has_side_effects=True, vmem_limit_bytes=32 * 1024 * 1024),
    )(*args)


def solution(mesh):
    placed = P(("parts", "gz"), "gx", "gy")
    sizes = {axis: mesh.shape[axis] for axis in ("gx", "gy", "gz")}
    return jax.shard_map(
        functools.partial(body, sizes),
        mesh=mesh,
        in_specs=(placed,) * 5 + (P(), P()),
        out_specs=(placed,) * 4,
        check_vma=False,
    )
```

time: 192 us -> 29.1 us (0.15)
  blocking collectives: 90.8 us -> 0 us
  waiting for transfers between devices: 45.7 us -> 0 us
  starting transfers between devices: 39.7 us -> 0 us
  Pallas kernels: 0 us -> 19.3 us
  other arithmetic: 9.56 us -> 0 us
  local copies, waits for them, and re-layouts: 0.8 us -> 8.86 us
  between operations: 5.13 us -> 0.66 us
    psum x3 -> x0, blocking collectives: 90.8 us -> none  [the longest x2 60.6 us: global_sum(): return lax.psum(jnp.sum(values), ('gx', 'gy', 'gz'))]
    ppermute x23 -> x0, waiting for transfers between devices: 45.7 us -> none  [the longest x11 38.3 us: with_halo(): after = lax.ppermute(leading, axis, down)]
    ppermute x23 -> x0, starting transfers between devices: 39.7 us -> none  [the longest x12 25.4 us: with_halo(): before = lax.ppermute(last, axis, up)]
    pallas_call x0 -> x1, Pallas kernels: none -> 19.3 us  [body(): pl.pallas_call(functools.partial(kernel, sizes, (lay, nx, ny)), out_shape...]
    unnamed x8 -> x18, local copies, waits for them, and re-layouts: 0.02 us -> 8.86 us
    reduce_sum x4 -> x0, other arithmetic: 4.44 us -> none  [the longest x2 2.18 us: body(): alpha = rho_now / lax.psum(jnp.sum(direction * result), ('gx', 'gy', 'gz'))]
  transfers between devices with their start and end apart: 23 -> 0, of which waited for: 17 -> 0; matrix products, arithmetic and copies ran while one was open for 0% -> 0% of each run, Pallas kernels for 0% -> 0%
where the time goes in v1:
time: 29.1 us; the launch traced here: 28.8 us
  Pallas kernels  19.3 us (66%)
  local copies, waits for them, and re-layouts  8.86 us (30%)
  between operations  0.66 us (2%)
    pallas_call x1, Pallas kernels, body(): pl.pallas_call(functools.partial(kernel, sizes, (lay, nx, ny)), out_shape...  19.3 us
    unnamed x18, local copies, waits for them, and re-layouts  8.86 us

profile of v1, /device:TPU:0, one launch (start us, length us, event | category | flops | bytes accessed | tf_op | source)
XLA Modules:
  0.0 28.8 jit_solution(5173031851883478180)
XLA Ops:
  0.6 0.0 copy-start
  0.6 0.9 %copy-done = f32[2,64,512]{2,1,0:T(8,128)S(1)} copy-done((f32[2,64,512]{2,1,0:T(8,128)S(1)}, f32[2,64,512]{2,1,0:T(8,128)}, u32[]{:S(2)}) %copy-start) | copy-done | bytes 262168
  1.6 0.0 copy-start.1
  1.6 0.9 %copy-done.1 = f32[2,64,512]{2,1,0:T(8,128)S(1)} copy-done((f32[2,64,512]{2,1,0:T(8,128)S(1)}, f32[2,64,512]{2,1,0:T(8,128)}, u32[]{:S(2)}) %copy-start.1) | copy-done | bytes 262168
  2.5 0.0 copy-start.2
  2.5 0.9 %copy-done.2 = s32[2,64,512]{2,1,0:T(8,128)S(1)} copy-done((s32[2,64,512]{2,1,0:T(8,128)S(1)}, s32[2,64,512]{2,1,0:T(8,128)}, u32[]{:S(2)}) %copy-start.2) | copy-done | bytes 262168
  3.5 0.0 copy-start.3
  3.5 0.9 %copy-done.3 = s32[2,64,512]{2,1,0:T(8,128)S(1)} copy-done((s32[2,64,512]{2,1,0:T(8,128)S(1)}, s32[2,64,512]{2,1,0:T(8,128)}, u32[]{:S(2)}) %copy-start.3) | copy-done | bytes 262168
  4.4 0.0 copy-start.4
  4.4 0.9 %copy-done.4 = f32[2,64,512]{2,1,0:T(8,128)S(1)} copy-done((f32[2,64,512]{2,1,0:T(8,128)S(1)}, f32[2,64,512]{2,1,0:T(8,128)}, u32[]{:S(2)}) %copy-start.4) | copy-done | bytes 262168
  5.4 0.0 copy-start.5
  5.4 0.7 %copy-done.5 = f32[4]{0:T(128)S(1)} copy-done((f32[4]{0:T(128)S(1)}, f32[4]{0:T(128)}, u32[]{:S(2)}) %copy-start.5) | copy-done | bytes 40
  6.0 0.0 copy-start.6
  6.0 0.7 %copy-done.6 = f32[8]{0:T(128)S(1)} copy-done((f32[8]{0:T(128)S(1)}, f32[8]{0:T(128)}, u32[]{:S(2)}) %copy-start.6) | copy-done | bytes 56
  6.7 19.3 %shard_map.102 = (f32[2,64,512]{2,1,0:T(8,128)S(1)}, f32[2,64,512]{2,1,0:T(8,128)S(1)}, f32[2,64,512]{2,1,0:T(8,128)S(1)}, f32[2,64,512]{2,1,0:T(8,128)S(1)}) custom-call(f32[2,64,512]{2,1,0:T(8,128)S(1)} %copy-done, f32[2,64,512]{2,1,0:T(8,128)S(1)} %copy-done.1, s32[2,64,512]{2,1,0:T(8,128)S(1)} %copy-done.2, s32[2,64,512]{2,1,0:T(8,128)S(1)} %copy-done.3, ...), custom_call_target="tpu_custom_call" | custom-call | tf_op jit(solution)/shard_map/pallas_call | solution.py:326
  26.0 0.7 %copy.15 = f32[2,64,512]{2,1,0:T(8,128)} copy(f32[2,64,512]{2,1,0:T(8,128)S(1)} %get-tuple-element.8) | data formatting | bytes 524288
  26.7 0.7 %copy.16 = f32[2,64,512]{2,1,0:T(8,128)} copy(f32[2,64,512]{2,1,0:T(8,128)S(1)} %get-tuple-element.9) | data formatting | bytes 524288
  27.4 0.7 %copy.17 = f32[2,64,512]{2,1,0:T(8,128)} copy(f32[2,64,512]{2,1,0:T(8,128)S(1)} %get-tuple-element.10) | data formatting | bytes 524288
  28.1 0.7 %copy.18 = f32[2,64,512]{2,1,0:T(8,128)} copy(f32[2,64,512]{2,1,0:T(8,128)S(1)} %get-tuple-element.11) | data formatting | bytes 524288
Async XLA Ops:
  0.6 1.0 %copy-start = (f32[2,64,512]{2,1,0:T(8,128)S(1)}, f32[2,64,512]{2,1,0:T(8,128)}, u32[]{:S(2)}) copy-start(f32[2,64,512]{2,1,0:T(8,128)} %source_hbm.1) | copy-start | bytes 786436
  1.6 0.9 %copy-start.1 = (f32[2,64,512]{2,1,0:T(8,128)S(1)}, f32[2,64,512]{2,1,0:T(8,128)}, u32[]{:S(2)}) copy-start(f32[2,64,512]{2,1,0:T(8,128)} %volt_hbm.1) | copy-start | bytes 786436
  2.5 0.9 %copy-start.2 = (s32[2,64,512]{2,1,0:T(8,128)S(1)}, s32[2,64,512]{2,1,0:T(8,128)}, u32[]{:S(2)}) copy-start(s32[2,64,512]{2,1,0:T(8,128)} %class_x_hbm.1) | copy-start | bytes 786436
  3.5 0.9 %copy-start.3 = (s32[2,64,512]{2,1,0:T(8,128)S(1)}, s32[2,64,512]{2,1,0:T(8,128)}, u32[]{:S(2)}) copy-start(s32[2,64,512]{2,1,0:T(8,128)} %class_y_hbm.1) | copy-start | bytes 786436
  4.4 0.9 %copy-start.4 = (f32[2,64,512]{2,1,0:T(8,128)S(1)}, f32[2,64,512]{2,1,0:T(8,128)}, u32[]{:S(2)}) copy-start(f32[2,64,512]{2,1,0:T(8,128)} %via_hbm.1) | copy-start | bytes 786436
  5.4 0.7 %copy-start.5 = (f32[4]{0:T(128)S(1)}, f32[4]{0:T(128)}, u32[]{:S(2)}) copy-start(f32[4]{0:T(128)} %sheet_ref.1) | copy-start | bytes 52
  6.0 0.7 %copy-start.6 = (f32[8]{0:T(128)S(1)}, f32[8]{0:T(128)}, u32[]{:S(2)}) copy-start(f32[8]{0:T(128)} %table_ref.1) | copy-start | bytes 100

commit v2 on v1

--- a/solution.py
+++ b/solution.py
@@ -314,16 +314,26 @@
     each_peer(lambda peer: share(peer, me).wait_send())
 
 
+def write_out(*refs):
+    sem = refs[-1]
+    copies = [pltpu.make_async_copy(refs[i], refs[4 + i], sem.at[i]) for i in range(4)]
+    for copy in copies:
+        copy.start()
+    for copy in copies:
+        copy.wait()
+
+
 def body(sizes, *args):
     lay, nx, ny = args[0].shape
     group = sizes["gx"] * sizes["gy"] * sizes["gz"]
     block = jax.ShapeDtypeStruct((lay, nx, ny), F32)
-    whole = pl.BlockSpec(memory_space=pl.ANY)
+    whole = pl.BlockSpec(memory_space=pltpu.HBM)
     scalars = pl.BlockSpec(memory_space=pltpu.SMEM)
     vmem = pl.BlockSpec(memory_space=pltpu.VMEM)
     flat = lambda dtype=F32: pltpu.VMEM((lay, nx, ny), dtype)
     tall = pltpu.VMEM((lay, nx + 2 * PAD, ny), F32)
-    return pl.pallas_call(
+    args = [pltpu.with_memory_space_constraint(a, pltpu.HBM) for a in args]
+    results = pl.pallas_call(
         functools.partial(kernel, sizes, (lay, nx, ny)),
         out_shape=(block,) * 4,
         in_specs=[whole] * 5 + [scalars] * 2,
@@ -342,6 +352,13 @@
         compiler_params=pltpu.CompilerParams(
             collective_id=0, has_side_effects=True, vmem_limit_bytes=32 * 1024 * 1024),
     )(*args)
+    return pl.pallas_call(
+        write_out,
+        out_shape=(block,) * 4,
+        in_specs=[pl.BlockSpec(memory_space=pl.ANY)] * 4, compiler_params=pltpu.CompilerParams(vmem_limit_bytes=1024*1024),
+        out_specs=(whole,) * 4,
+        scratch_shapes=[pltpu.SemaphoreType.DMA((4,))],
+    )(*results)
 
 
 def solution(mesh):

time: 29.1 us -> 21.1 us (0.73)
  local copies, waits for them, and re-layouts: 8.86 us -> 0 us
  Pallas kernels: 19.3 us -> 20.3 us
    unnamed x18 -> x0, local copies, waits for them, and re-layouts: 8.86 us -> none
    pallas_call x0 -> x1, Pallas kernels: none -> 1 us  [body(): pl.pallas_call(write_out, out_shape=(block,) * 4, in_specs=[pl.BlockSpec(...]
where the time goes in v2:
time: 21.1 us; the launch traced here: 20.9 us
  Pallas kernels  20.3 us (96%)
  between operations  0.64 us (3%)
    pallas_call x1, Pallas kernels, body(): pl.pallas_call(functools.partial(kernel, sizes, (lay, nx, ny)), out_shape...  19.3 us
    pallas_call x1, Pallas kernels, body(): pl.pallas_call(write_out, out_shape=(block,) * 4, in_specs=[pl.BlockSpec(...  1 us

profile of v2, /device:TPU:0, one launch (start us, length us, event | category | flops | bytes accessed | tf_op | source)
XLA Modules:
  0.0 20.9 jit_solution(6037540838708735077)
XLA Ops:
  0.6 19.3 %shard_map.102 = (f32[2,64,512]{2,1,0:T(8,128)S(1)}, f32[2,64,512]{2,1,0:T(8,128)S(1)}, f32[2,64,512]{2,1,0:T(8,128)S(1)}, f32[2,64,512]{2,1,0:T(8,128)S(1)}) custom-call(f32[2,64,512]{2,1,0:T(8,128)} %source_hbm.1, f32[2,64,512]{2,1,0:T(8,128)} %volt_hbm.1, s32[2,64,512]{2,1,0:T(8,128)} %class_x_hbm.1, s32[2,64,512]{2,1,0:T(8,128)} %class_y_hbm.1, ...), custom_call_target="tpu_custom_call" | custom-call | tf_op jit(solution)/shard_map/pallas_call | solution.py:336
  19.9 1.0 %shard_map.103 = (f32[2,64,512]{2,1,0:T(8,128)}, f32[2,64,512]{2,1,0:T(8,128)}, f32[2,64,512]{2,1,0:T(8,128)}, f32[2,64,512]{2,1,0:T(8,128)}) custom-call(f32[2,64,512]{2,1,0:T(8,128)S(1)} %get-tuple-element.8.refs_0_, f32[2,64,512]{2,1,0:T(8,128)S(1)} %get-tuple-element.9.refs_1_, f32[2,64,512]{2,1,0:T(8,128)S(1)} %get-tuple-element.10.refs_2_, ...), custom_call_target="tpu_custom_call" | custom-call | tf_op jit(solution)/shard_map/pallas_call | solution.py:355

commit v3 on v2

--- a/solution.py
+++ b/solution.py
@@ -12,12 +12,14 @@
 ROWS = 16
 LANES = 128
 MESSAGES = {
-    "cx": ("gx", 1), "cy": ("gy", 1), "cv": ("gz", 1),
-    "vx": ("gx", -1), "vy": ("gy", -1), "vl": ("gz", -1),
-    "zx_up": ("gx", 1), "zx_dn": ("gx", -1),
-    "zy_up": ("gy", 1), "zy_dn": ("gy", -1),
-    "zl_up": ("gz", 1), "zl_dn": ("gz", -1),
-    "tx": ("gx", -1), "ty": ("gy", -1), "tl": ("gz", -1),
+    "cx": {"gx": 1}, "cy": {"gy": 1}, "cv": {"gz": 1},
+    "vx": {"gx": -1}, "vy": {"gy": -1}, "vl": {"gz": -1},
+    "zx_up": {"gx": 1}, "zy_up": {"gy": 1}, "zl_up": {"gz": 1}, "zl_dn": {"gz": -1},
+    "xd": {"gx": -1}, "yd": {"gy": -1}, "tl": {"gz": -1},
+    "lx_up": {"gx": -1, "gz": 1}, "lx_dn": {"gx": -1, "gz": -1},
+    "ly_up": {"gy": -1, "gz": 1}, "ly_dn": {"gy": -1, "gz": -1},
+    "ca": {"gx": -1, "gy": 1}, "cb": {"gx": -1, "gy": -1}, "cc": {"gx": -1, "gy": -1},
+    "cd": {"gx": 1, "gy": -1},
 }
 NAMES = list(MESSAGES)
 
@@ -27,7 +29,9 @@
     source_hbm, volt_hbm, class_x_hbm, class_y_hbm, via_hbm, sheet_ref, table_ref,
     adj_ref, grad_x_ref, grad_y_ref, grad_v_ref,
     source, volt, class_x, class_y, via, cond_x, cond_y, low_y, inverse, z, t, adj,
-    row_send, row_recv, col_send, col_recv, lay_recv, part, parts,
+    row_send, row_recv, col_send, col_recv, lay_recv,
+    xd_send, xd_recv, yd_send, yd_recv, over_send, over_recv, row_end_send, row_end_recv,
+    col_end_send, col_end_recv, part, parts,
     load_sem, send_sem, recv_sem, part_send, part_recv,
 ):
     lay, nx, ny = dims
@@ -49,6 +53,10 @@
     row_recv[...] = jnp.zeros_like(row_recv)
     col_recv[...] = jnp.zeros_like(col_recv)
     lay_recv[...] = jnp.zeros_like(lay_recv)
+    for ref in (xd_recv, yd_recv, over_recv, row_end_recv, col_end_recv):
+        ref[...] = jnp.zeros_like(ref)
+    z[:, PAD - 1, :] = jnp.zeros((lay, ny), F32)
+    z[:, last + 1, :] = jnp.zeros((lay, ny), F32)
 
     def place(rank):
         gz = lax.rem(rank, sizes["gz"])
@@ -67,59 +75,73 @@
     each_peer(lambda peer: pl.semaphore_signal(
         barrier, inc=1, device_id=place(peer), device_id_type=pl.DeviceIdType.MESH))
 
-    ROW = {"cx": 0, "vx": 1, "zx_up": 2, "zx_dn": 3, "tx": 4}
-    COL = {"cy": 0, "vy": 1, "zy_up": 2, "zy_dn": 3, "ty": 4}
+    ROW = {"cx": 0, "vx": 1, "zx_up": 2}
+    COL = {"cy": 0, "vy": 1, "zy_up": 2, "ly_up": 3, "ly_dn": 4}
     LAY = {"cv": 0, "vl": 1, "zl_up": 2, "zl_dn": 3, "tl": 4}
     LAY_SRC = {
         "cv": via.at[lay - 1], "vl": volt.at[0, inner, :], "zl_up": z.at[lay - 1, inner, :],
         "zl_dn": z.at[0, inner, :], "tl": t.at[0, inner, :],
     }
 
+    OTHER = {
+        "xd": (xd_send, xd_recv), "yd": (yd_send, yd_recv),
+        "lx_up": (over_send.at[0], over_recv.at[0]), "lx_dn": (over_send.at[1], over_recv.at[1]),
+        "ca": (row_end_send.at[0], row_end_recv.at[0]), "cb": (row_end_send.at[1], row_end_recv.at[1]),
+        "cc": (col_end_send.at[0], col_end_recv.at[0]), "cd": (col_end_send.at[1], col_end_recv.at[1]),
+    }
+
     def message(name):
-        axis, way = MESSAGES[name]
         i = NAMES.index(name)
         if name in ROW:
             src, dst = row_send.at[ROW[name]], row_recv.at[ROW[name]]
         elif name in COL:
             src, dst = col_send.at[COL[name]], col_recv.at[COL[name]]
+        elif name in OTHER:
+            src, dst = OTHER[name]
         else:
             src, dst = LAY_SRC[name], lay_recv.at[LAY[name]]
-        size = sizes[axis]
-        to = lax.rem(here[axis] + (way + size), size)
+        to = {axis: lax.rem(here[axis] + (way + sizes[axis]), sizes[axis])
+              for axis, way in MESSAGES[name].items()}
         return pltpu.make_async_remote_copy(
             src_ref=src, dst_ref=dst, send_sem=send_sem.at[i], recv_sem=recv_sem.at[i],
-            device_id={axis: to}, device_id_type=pl.DeviceIdType.MESH)
+            device_id=to, device_id_type=pl.DeviceIdType.MESH)
 
     def at_end(axis, way):
         return here[axis] == (sizes[axis] - 1 if way > 0 else 0)
 
+    def guarded(name, sign, action):
+        ways = MESSAGES[name]
+        if any(sizes[axis] == 1 for axis in ways):
+            return
+        inside = [jnp.logical_not(at_end(axis, sign * way)) for axis, way in ways.items()]
+        pl.when(functools.reduce(jnp.logical_and, inside))(action)
+
     def send(*names):
         for name in names:
-            axis, way = MESSAGES[name]
-            if sizes[axis] > 1:
-                pl.when(jnp.logical_not(at_end(axis, way)))(message(name).start)
+            guarded(name, 1, message(name).start)
 
     def receive(*names):
         for name in names:
-            axis, way = MESSAGES[name]
-            if sizes[axis] > 1:
-                pl.when(jnp.logical_not(at_end(axis, -way)))(message(name).wait_recv)
+            guarded(name, -1, message(name).wait_recv)
 
     def sent(*names):
         for name in names:
-            axis, way = MESSAGES[name]
-            if sizes[axis] > 1:
-                pl.when(jnp.logical_not(at_end(axis, way)))(message(name).wait_send)
+            guarded(name, 1, message(name).wait_send)
 
     chunks = [(l, r) for l in range(lay) for r in range(0, nx, ROWS)]
     lane = lax.broadcasted_iota(jnp.int32, (ROWS, LANES), 1)
 
+    def as_row(tile, at):
+        return tile.reshape(lay * nx, LANES).T[at:at + 1, :]
+
     def put_col(name, tile, at):
-        col_send[COL[name]] = tile.reshape(lay * nx, LANES).T[at:at + 1, :]
+        col_send[COL[name]] = as_row(tile, at)
+
+    def as_col(row):
+        return jnp.broadcast_to(row, (LANES, lay * nx)).T
 
     def col_halo(name):
-        row = col_recv[COL[name]]
-        return jnp.broadcast_to(row, (LANES, lay * nx)).T
+        return as_col(col_recv[COL[name]])
 
     def from_left(value, edge):
         moved = pltpu.roll(value, 1, 1)
@@ -190,10 +212,59 @@
         z[l, PAD + r:PAD + r + ROWS, :] = value
         moment0 = moment0 + source[l, rows, :] * value
     row_send[ROW["zx_up"]] = z[:, last, :]
-    row_send[ROW["zx_dn"]] = z[:, first, :]
     put_col("zy_up", z[:, inner, ny - LANES:], LANES - 1)
-    put_col("zy_dn", z[:, inner, :LANES], 0)
-    send("zl_up", "zl_dn", "zx_up", "zx_dn", "zy_up", "zy_dn")
+    send("zl_up", "zl_dn", "zx_up", "zy_up")
+
+    one = lane[0:1]
+
+    def from_left_row(value):
+        moved = pltpu.roll(value, 1, 1)
+        return jnp.concatenate([jnp.where(one == 0, 0.0, moved[:, :LANES]), moved[:, LANES:]], axis=1)
+
+    def from_right_row(value):
+        moved = pltpu.roll(value, ny - 1, 1)
+        tail = jnp.where(one == LANES - 1, 0.0, moved[:, ny - LANES:])
+        return jnp.concatenate([moved[:, :ny - LANES], tail], axis=1)
+
+    col_parts = []
+    for l in range(lay):
+        row = z[l, first:first + 1, :]
+        s = cond_x[l, first:first + 1, :] * z[l, first + 1:first + 2, :]
+        s = s + cond_y[l, 0:1, :] * from_right_row(row) + low_y[l, 0:1, :] * from_left_row(row)
+        tile = z[l, inner, :LANES]
+        c = cond_x[l, inner, :LANES] * z[l, PAD + 1:PAD + 1 + nx, :LANES]
+        c = c + cond_x[l, PAD - 1:PAD - 1 + nx, :LANES] * z[l, PAD - 1:PAD - 1 + nx, :LANES]
+        c = c + cond_y[l, :, :LANES] * pltpu.roll(tile, LANES - 1, 1)
+        if l + 1 < lay:
+            s = s + via[l, 0:1, :] * z[l + 1, first:first + 1, :]
+            c = c + via[l, :, :LANES] * z[l + 1, inner, :LANES]
+        if l > 0:
+            s = s + via[l - 1, 0:1, :] * z[l - 1, first:first + 1, :]
+            c = c + via[l - 1, :, :LANES] * z[l - 1, inner, :LANES]
+        xd_send[l:l + 1, :] = row
+        xd_send[lay + l:lay + l + 1, :] = s
+        xd_send[2 * lay + l:2 * lay + l + 1, :] = inverse[l, 0:1, :]
+        col_parts.append(c)
+    yd_send[0:1, :] = as_row(z[:, inner, :LANES], 0)
+    yd_send[1:2, :] = as_row(jnp.stack(col_parts), 0)
+    yd_send[2:3, :] = as_row(inverse[:, :, :LANES], 0)
+    top = lay - 1
+    over_send[0] = via[top, 0:1, :] * z[top, first:first + 1, :]
+    over_send[1] = lay_recv[LAY["cv"], 0:1, :] * z[0, first:first + 1, :]
+    blank = [jnp.zeros((nx, LANES), F32)] * (lay - 1)
+    put_col("ly_up", jnp.stack([via[top, :, :LANES] * z[top, inner, :LANES]] + blank), 0)
+    put_col("ly_dn", jnp.stack(blank + [lay_recv[LAY["cv"], :, :LANES] * z[0, inner, :LANES]]), 0)
+    for l in range(lay):
+        row = z[l, first:first + 1, :]
+        tail = cond_y[l, 0:1, ny - LANES:] * row[:, ny - LANES:]
+        row_end_send[0, l:l + 1, :] = jnp.where(one == 0, pltpu.roll(tail, 1, 1), 0.0)
+        head = low_y[l, 0:1, :LANES] * row[:, :LANES]
+        row_end_send[1, l:l + 1, :] = jnp.where(one == LANES - 1, pltpu.roll(head, LANES - 1, 1), 0.0)
+        head = cond_x[l, PAD - 1:PAD, :LANES] * row[:, :LANES]
+        col_end_send[0, l:l + 1, :] = jnp.broadcast_to(head[:, :1], (1, lay * nx))
+        head = cond_x[l, last:last + 1, :LANES] * z[l, last:last + 1, :LANES]
+        col_end_send[1, l:l + 1, :] = jnp.broadcast_to(head[:, :1], (1, lay * nx))
+    send("xd", "yd", "lx_up", "lx_dn", "ly_up", "ly_dn", "ca", "cb", "cc", "cd")
 
     receive("vx", "vy", "vl")
     volt[:, last + 1, :] = row_recv[ROW["vx"]]
@@ -217,11 +288,11 @@
             spot = lax.broadcasted_iota(jnp.int32, tile.shape, 1)
             grad_y_ref[l, :, ny - LANES:] = jnp.where(spot == LANES - 1, 0.0, tile)
 
-    receive("zx_up", "zx_dn", "zy_up", "zy_dn", "zl_up", "zl_dn")
+    receive("zx_up", "zy_up", "zl_up", "zl_dn", "xd", "yd")
     z[:, PAD - 1, :] = row_recv[ROW["zx_up"]]
-    z[:, last + 1, :] = row_recv[ROW["zx_dn"]]
+    z[:, last + 1, :] = xd_recv[:lay, :]
     halo_lo = col_halo("zy_up")
-    halo_hi = col_halo("zy_dn")
+    halo_hi = as_col(yd_recv[0:1, :])
     moment1 = jnp.zeros((ROWS, ny), F32)
     moment2 = jnp.zeros((ROWS, ny), F32)
     for l, r in chunks:
@@ -241,12 +312,27 @@
         t[l, mid, :] = value
         moment1 = moment1 + here_z * s
         moment2 = moment2 + value * s
-    row_send[ROW["tx"]] = t[:, first, :]
-    put_col("ty", t[:, inner, :LANES], 0)
-    send("tl", "tx", "ty")
-    receive("tx", "ty", "tl")
-    t[:, last + 1, :] = row_recv[ROW["tx"]]
-    halo_t = col_halo("ty")
+    send("tl")
+
+    receive("lx_up", "lx_dn", "ly_up", "ly_dn", "ca", "cb", "cc", "cd")
+    for l in range(lay):
+        s = xd_recv[lay + l:lay + l + 1, :] + cond_x[l, last:last + 1, :] * z[l, last:last + 1, :]
+        if l == 0:
+            s = s + over_recv[0]
+        if l == lay - 1:
+            s = s + over_recv[1]
+        s = jnp.concatenate(
+            [s[:, :LANES] + row_end_recv[0, l:l + 1, :], s[:, LANES:ny - LANES],
+             s[:, ny - LANES:] + row_end_recv[1, l:l + 1, :]], axis=1)
+        t[l, last + 1:last + 2, :] = s * xd_recv[2 * lay + l:2 * lay + l + 1, :]
+    s = yd_recv[1:2, :] + col_send[COL["cy"]] * col_send[COL["zy_up"]]
+    s = s + col_recv[COL["ly_up"]] + col_recv[COL["ly_dn"]]
+    spot = lax.broadcasted_iota(jnp.int32, (1, lay * nx), 1)
+    for l in range(lay):
+        s = s + jnp.where(spot == l * nx + nx - 1, col_end_recv[0, l:l + 1, :], 0.0)
+        s = s + jnp.where(spot == l * nx, col_end_recv[1, l:l + 1, :], 0.0)
+    halo_t = as_col(s * yd_recv[2:3, :])
+    receive("tl")
     moment3 = jnp.zeros((ROWS, ny), F32)
     for l, r in chunks:
         rows = slice(r, r + ROWS)
@@ -341,9 +427,14 @@
         scratch_shapes=[
             flat(), tall, flat(jnp.int32), flat(jnp.int32), flat(),
             tall, flat(), flat(), flat(), tall, tall, tall,
-            pltpu.VMEM((5, lay, ny), F32), pltpu.VMEM((5, lay, ny), F32),
+            pltpu.VMEM((3, lay, ny), F32), pltpu.VMEM((3, lay, ny), F32),
             pltpu.VMEM((5, 1, lay * nx), F32), pltpu.VMEM((5, 1, lay * nx), F32),
             pltpu.VMEM((5, nx, ny), F32),
+            pltpu.VMEM((3 * lay, ny), F32), pltpu.VMEM((3 * lay, ny), F32),
+            pltpu.VMEM((3, lay * nx), F32), pltpu.VMEM((3, lay * nx), F32),
+            pltpu.VMEM((2, 1, ny), F32), pltpu.VMEM((2, 1, ny), F32),
+            pltpu.VMEM((2, lay, LANES), F32), pltpu.VMEM((2, lay, LANES), F32),
+            pltpu.VMEM((2, lay, lay * nx), F32), pltpu.VMEM((2, lay, lay * nx), F32),
             pltpu.VMEM((8, LANES), F32), pltpu.VMEM((group, 8, LANES), F32),
             pltpu.SemaphoreType.DMA((5,)),
             pltpu.SemaphoreType.DMA((len(NAMES),)), pltpu.SemaphoreType.DMA((len(NAMES),)),

time: 21.1 us -> 19.2 us (0.910)
  Pallas kernels: 20.3 us -> 18.3 us
    pallas_call x1, Pallas kernels: 19.3 us -> 17.3 us  [body(): pl.pallas_call(functools.partial(kernel, sizes, (lay, nx, ny)), out_shape...]
where the time goes in v3:
time: 19.2 us; the launch traced here: 19 us
  Pallas kernels  18.3 us (95%)
  between operations  0.64 us (3%)
    pallas_call x1, Pallas kernels, body(): pl.pallas_call(functools.partial(kernel, sizes, (lay, nx, ny)), out_shape...  17.3 us
    pallas_call x1, Pallas kernels, body(): pl.pallas_call(write_out, out_shape=(block,) * 4, in_specs=[pl.BlockSpec(...  1 us

profile of v3, /device:TPU:0, one launch (start us, length us, event | category | flops | bytes accessed | tf_op | source)
XLA Modules:
  0.0 19.0 jit_solution(12694612554609313531)
XLA Ops:
  0.6 17.3 %shard_map.102 = (f32[2,64,512]{2,1,0:T(8,128)S(1)}, f32[2,64,512]{2,1,0:T(8,128)S(1)}, f32[2,64,512]{2,1,0:T(8,128)S(1)}, f32[2,64,512]{2,1,0:T(8,128)S(1)}) custom-call(f32[2,64,512]{2,1,0:T(8,128)} %source_hbm.1, f32[2,64,512]{2,1,0:T(8,128)} %volt_hbm.1, s32[2,64,512]{2,1,0:T(8,128)} %class_x_hbm.1, s32[2,64,512]{2,1,0:T(8,128)} %class_y_hbm.1, ...), custom_call_target="tpu_custom_call" | custom-call | tf_op jit(solution)/shard_map/pallas_call | solution.py:422
  18.0 1.0 %shard_map.103 = (f32[2,64,512]{2,1,0:T(8,128)}, f32[2,64,512]{2,1,0:T(8,128)}, f32[2,64,512]{2,1,0:T(8,128)}, f32[2,64,512]{2,1,0:T(8,128)}) custom-call(f32[2,64,512]{2,1,0:T(8,128)S(1)} %get-tuple-element.8.refs_0_, f32[2,64,512]{2,1,0:T(8,128)S(1)} %get-tuple-element.9.refs_1_, f32[2,64,512]{2,1,0:T(8,128)S(1)} %get-tuple-element.10.refs_2_, ...), custom_call_target="tpu_custom_call" | custom-call | tf_op jit(solution)/shard_map/pallas_call | solution.py:446

commit v4 on v3

--- a/solution.py
+++ b/solution.py
@@ -28,7 +28,7 @@
     sizes, dims,
     source_hbm, volt_hbm, class_x_hbm, class_y_hbm, via_hbm, sheet_ref, table_ref,
     adj_ref, grad_x_ref, grad_y_ref, grad_v_ref,
-    source, volt, class_x, class_y, via, cond_x, cond_y, low_y, inverse, z, t, adj,
+    source, volt, class_x, class_y, via, cond_x, cond_y, low_y, inverse, z, t, of_t,
     row_send, row_recv, col_send, col_recv, lay_recv,
     xd_send, xd_recv, yd_send, yd_recv, over_send, over_recv, row_end_send, row_end_recv,
     col_end_send, col_end_recv, part, parts,
@@ -52,11 +52,22 @@
 
     row_recv[...] = jnp.zeros_like(row_recv)
     col_recv[...] = jnp.zeros_like(col_recv)
-    lay_recv[...] = jnp.zeros_like(lay_recv)
     for ref in (xd_recv, yd_recv, over_recv, row_end_recv, col_end_recv):
         ref[...] = jnp.zeros_like(ref)
     z[:, PAD - 1, :] = jnp.zeros((lay, ny), F32)
     z[:, last + 1, :] = jnp.zeros((lay, ny), F32)
+
+    empty = jnp.zeros((nx, ny), F32)
+
+    @pl.when(here["gz"] == sizes["gz"] - 1)
+    def _():
+        for slot in (1, 3, 4):
+            lay_recv[slot] = empty
+
+    @pl.when(here["gz"] == 0)
+    def _():
+        for slot in (0, 2):
+            lay_recv[slot] = empty
 
     def place(rank):
         gz = lax.rem(rank, sizes["gz"])
@@ -312,7 +323,8 @@
         t[l, mid, :] = value
         moment1 = moment1 + here_z * s
         moment2 = moment2 + value * s
-    send("tl")
+        if l == 0 and r + ROWS == nx:
+            send("tl")
 
     receive("lx_up", "lx_dn", "ly_up", "ly_dn", "ca", "cb", "cc", "cd")
     for l in range(lay):
@@ -332,18 +344,22 @@
         s = s + jnp.where(spot == l * nx + nx - 1, col_end_recv[0, l:l + 1, :], 0.0)
         s = s + jnp.where(spot == l * nx, col_end_recv[1, l:l + 1, :], 0.0)
     halo_t = as_col(s * yd_recv[2:3, :])
-    receive("tl")
     moment3 = jnp.zeros((ROWS, ny), F32)
     for l, r in chunks:
         rows = slice(r, r + ROWS)
         mid = slice(PAD + r, PAD + r + ROWS)
         upper = slice(PAD + 1 + r, PAD + 1 + r + ROWS)
         here_t = t[l, mid, :]
-        t_above = t[l + 1, mid, :] if l + 1 < lay else lay_recv[LAY["tl"], rows, :]
         s = cond_x[l, mid, :] * t[l, upper, :]
         s = s + cond_y[l, rows, :] * from_right(here_t, edge_of(halo_t, l, r))
-        s = s + via[l, rows, :] * t_above
+        if l + 1 < lay:
+            s = s + via[l, rows, :] * t[l + 1, mid, :]
         moment3 = moment3 + here_t * s
+    receive("tl")
+    for r in range(0, nx, ROWS):
+        rows = slice(r, r + ROWS)
+        s = via[lay - 1, rows, :] * lay_recv[LAY["tl"], rows, :]
+        moment3 = moment3 + t[lay - 1, PAD + r:PAD + r + ROWS, :] * s
 
     def fold(value):
         wide = sum(value[:, k:k + LANES] for k in range(0, ny, LANES))
@@ -362,6 +378,26 @@
 
     each_peer(lambda peer: share(peer, me).start())
     parts[me] = part[...]
+
+    for l, r in chunks:
+        rows = slice(r, r + ROWS)
+        mid = slice(PAD + r, PAD + r + ROWS)
+        upper = slice(PAD + 1 + r, PAD + 1 + r + ROWS)
+        here_z, here_t = z[l, mid, :], t[l, mid, :]
+        if l + 1 < lay:
+            z_above, t_above = z[l + 1, mid, :], t[l + 1, mid, :]
+        else:
+            z_above, t_above = lay_recv[LAY["zl_dn"], rows, :], lay_recv[LAY["tl"], rows, :]
+        volts = grad_x_ref[l, rows, :]
+        grad_x_ref[l, rows, :] = volts * (here_z - z[l, upper, :])
+        of_t[0, l, rows, :] = volts * (here_t - t[l, upper, :])
+        volts = grad_y_ref[l, rows, :]
+        grad_y_ref[l, rows, :] = volts * (here_z - from_right(here_z, edge_of(halo_hi, l, r)))
+        of_t[1, l, rows, :] = volts * (here_t - from_right(here_t, edge_of(halo_t, l, r)))
+        volts = grad_v_ref[l, rows, :]
+        grad_v_ref[l, rows, :] = volts * (here_z - z_above)
+        of_t[2, l, rows, :] = volts * (here_t - t_above)
+
     each_peer(lambda peer: share(peer, peer).wait_recv())
     totals = jnp.sum(jnp.sum(parts[...], axis=0), axis=1, keepdims=True)
     c0, c1, c2, c3 = (totals[k:k + 1, :] for k in range(4))
@@ -376,25 +412,12 @@
     factor_z = jnp.broadcast_to(alpha + alpha_next * (rest + beta), (1, ny))
     factor_t = jnp.broadcast_to(alpha_next * alpha, (1, ny))
 
-    adj[:, last + 1, :] = factor_z * z[:, last + 1, :] + factor_t * t[:, last + 1, :]
-    for l, r in chunks:
+    for l, r in chunks:
+        rows = slice(r, r + ROWS)
         mid = slice(PAD + r, PAD + r + ROWS)
-        value = factor_z * z[l, mid, :] + factor_t * t[l, mid, :]
-        adj[l, mid, :] = value
-        adj_ref[l, r:r + ROWS, :] = value
-    halo = factor_z[:, :LANES] * halo_hi + factor_t[:, :LANES] * halo_t
-    for l, r in chunks:
-        rows = slice(r, r + ROWS)
-        mid = slice(PAD + r, PAD + r + ROWS)
-        upper = slice(PAD + 1 + r, PAD + 1 + r + ROWS)
-        value = adj[l, mid, :]
-        if l + 1 < lay:
-            above = adj[l + 1, mid, :]
-        else:
-            above = factor_z * lay_recv[LAY["zl_dn"], rows, :] + factor_t * lay_recv[LAY["tl"], rows, :]
-        grad_x_ref[l, rows, :] = grad_x_ref[l, rows, :] * (value - adj[l, upper, :])
-        grad_y_ref[l, rows, :] = grad_y_ref[l, rows, :] * (value - from_right(value, edge_of(halo, l, r)))
-        grad_v_ref[l, rows, :] = grad_v_ref[l, rows, :] * (value - above)
+        adj_ref[l, rows, :] = factor_z * z[l, mid, :] + factor_t * t[l, mid, :]
+        for k, ref in enumerate((grad_x_ref, grad_y_ref, grad_v_ref)):
+            ref[l, rows, :] = factor_z * ref[l, rows, :] + factor_t * of_t[k, l, rows, :]
 
     sent(*NAMES)
     each_peer(lambda peer: share(peer, me).wait_send())
@@ -426,7 +449,7 @@
         out_specs=(vmem,) * 4,
         scratch_shapes=[
             flat(), tall, flat(jnp.int32), flat(jnp.int32), flat(),
-            tall, flat(), flat(), flat(), tall, tall, tall,
+            tall, flat(), flat(), flat(), tall, tall, pltpu.VMEM((3, lay, nx, ny), F32),
             pltpu.VMEM((3, lay, ny), F32), pltpu.VMEM((3, lay, ny), F32),
             pltpu.VMEM((5, 1, lay * nx), F32), pltpu.VMEM((5, 1, lay * nx), F32),
             pltpu.VMEM((5, nx, ny), F32),

time: 19.2 us -> 19.1 us (level)
  no operation moved by 1% of the time
where the time goes in v4:
time: 19.1 us; the launch traced here: 18.9 us
  Pallas kernels  18.3 us (96%)
  between operations  0.64 us (3%)
    pallas_call x1, Pallas kernels, body(): pl.pallas_call(functools.partial(kernel, sizes, (lay, nx, ny)), out_shape...  17.3 us
    pallas_call x1, Pallas kernels, body(): pl.pallas_call(write_out, out_shape=(block,) * 4, in_specs=[pl.BlockSpec(...  1 us

profile of v4, /device:TPU:0, one launch (start us, length us, event | category | flops | bytes accessed | tf_op | source)
XLA Modules:
  0.0 18.9 jit_solution(3872805740459910523)
XLA Ops:
  0.6 17.3 %shard_map.102 = (f32[2,64,512]{2,1,0:T(8,128)S(1)}, f32[2,64,512]{2,1,0:T(8,128)S(1)}, f32[2,64,512]{2,1,0:T(8,128)S(1)}, f32[2,64,512]{2,1,0:T(8,128)S(1)}) custom-call(f32[2,64,512]{2,1,0:T(8,128)} %source_hbm.1, f32[2,64,512]{2,1,0:T(8,128)} %volt_hbm.1, s32[2,64,512]{2,1,0:T(8,128)} %class_x_hbm.1, s32[2,64,512]{2,1,0:T(8,128)} %class_y_hbm.1, ...), custom_call_target="tpu_custom_call" | custom-call | tf_op jit(solution)/shard_map/pallas_call | solution.py:445
  17.9 1.0 %shard_map.103 = (f32[2,64,512]{2,1,0:T(8,128)}, f32[2,64,512]{2,1,0:T(8,128)}, f32[2,64,512]{2,1,0:T(8,128)}, f32[2,64,512]{2,1,0:T(8,128)}) custom-call(f32[2,64,512]{2,1,0:T(8,128)S(1)} %get-tuple-element.8.refs_0_, f32[2,64,512]{2,1,0:T(8,128)S(1)} %get-tuple-element.9.refs_1_, f32[2,64,512]{2,1,0:T(8,128)S(1)} %get-tuple-element.10.refs_2_, ...), custom_call_target="tpu_custom_call" | custom-call | tf_op jit(solution)/shard_map/pallas_call | solution.py:469

commit v5 on v4

--- a/solution.py
+++ b/solution.py
@@ -78,7 +78,7 @@
 
     def each_peer(body):
         if group <= 32:
-            for k in range(1, group):
+            for k in sorted(range(1, group), key=lambda k: -min(k, group - k)):
                 body(lax.rem(me + k, group))
         else:
             lax.fori_loop(1, group, lambda k, c: (body(lax.rem(me + k, group)), c)[1], 0)
@@ -361,15 +361,18 @@
         s = via[lay - 1, rows, :] * lay_recv[LAY["tl"], rows, :]
         moment3 = moment3 + t[lay - 1, PAD + r:PAD + r + ROWS, :] * s
 
+    quarter = LANES // 4
+
     def fold(value):
         wide = sum(value[:, k:k + LANES] for k in range(0, ny, LANES))
-        return jnp.sum(wide, axis=0, keepdims=True)
-
-    part[0:1, :] = fold(moment0)
-    part[1:2, :] = fold(moment1)
-    part[2:3, :] = fold(moment2)
-    part[3:4, :] = 2.0 * fold(moment3)
-    part[4:8, :] = jnp.zeros((4, LANES), F32)
+        line = jnp.sum(wide, axis=0, keepdims=True)
+        line = line + pltpu.roll(line, 2 * quarter, 1)
+        return line + pltpu.roll(line, quarter, 1)
+
+    packed = 2.0 * fold(moment3)
+    for k, moment in ((2, moment2), (1, moment1), (0, moment0)):
+        packed = jnp.where(one < (k + 1) * quarter, fold(moment), packed)
+    part[...] = packed
 
     def share(peer, slot):
         return pltpu.make_async_remote_copy(
@@ -399,7 +402,11 @@
         of_t[2, l, rows, :] = volts * (here_t - t_above)
 
     each_peer(lambda peer: share(peer, peer).wait_recv())
-    totals = jnp.sum(jnp.sum(parts[...], axis=0), axis=1, keepdims=True)
+    summed = jnp.broadcast_to(jnp.sum(parts[...], axis=0), (8, LANES))
+    spot = lax.broadcasted_iota(jnp.int32, (8, LANES), 1)
+    low = lax.broadcasted_iota(jnp.int32, (8, LANES), 0) * quarter
+    mine = jnp.logical_and(spot >= low, spot < low + quarter)
+    totals = jnp.sum(jnp.where(mine, summed, 0.0), axis=1, keepdims=True)
     c0, c1, c2, c3 = (totals[k:k + 1, :] for k in range(4))
     curve = c0 - c1
     alpha = c0 / curve
@@ -458,7 +465,7 @@
             pltpu.VMEM((2, 1, ny), F32), pltpu.VMEM((2, 1, ny), F32),
             pltpu.VMEM((2, lay, LANES), F32), pltpu.VMEM((2, lay, LANES), F32),
             pltpu.VMEM((2, lay, lay * nx), F32), pltpu.VMEM((2, lay, lay * nx), F32),
-            pltpu.VMEM((8, LANES), F32), pltpu.VMEM((group, 8, LANES), F32),
+            pltpu.VMEM((1, LANES), F32), pltpu.VMEM((group, 1, LANES), F32),
             pltpu.SemaphoreType.DMA((5,)),
             pltpu.SemaphoreType.DMA((len(NAMES),)), pltpu.SemaphoreType.DMA((len(NAMES),)),
             pltpu.SemaphoreType.DMA((group,)), pltpu.SemaphoreType.DMA((group,)),

time: 19.1 us -> 18.9 us (0.990)
  Pallas kernels: 18.3 us -> 18.1 us
where the time goes in v5:
time: 18.9 us; the launch traced here: 18.7 us
  Pallas kernels  18.1 us (96%)
  between operations  0.64 us (3%)
    pallas_call x1, Pallas kernels, body(): pl.pallas_call(functools.partial(kernel, sizes, (lay, nx, ny)), out_shape...  17.1 us
    pallas_call x1, Pallas kernels, body(): pl.pallas_call(write_out, out_shape=(block,) * 4, in_specs=[pl.BlockSpec(...  1 us

profile of v5, /device:TPU:0, one launch (start us, length us, event | category | flops | bytes accessed | tf_op | source)
XLA Modules:
  0.0 18.7 jit_solution(14881410784340226753)
XLA Ops:
  0.6 17.1 %shard_map.102 = (f32[2,64,512]{2,1,0:T(8,128)S(1)}, f32[2,64,512]{2,1,0:T(8,128)S(1)}, f32[2,64,512]{2,1,0:T(8,128)S(1)}, f32[2,64,512]{2,1,0:T(8,128)S(1)}) custom-call(f32[2,64,512]{2,1,0:T(8,128)} %source_hbm.1, f32[2,64,512]{2,1,0:T(8,128)} %volt_hbm.1, s32[2,64,512]{2,1,0:T(8,128)} %class_x_hbm.1, s32[2,64,512]{2,1,0:T(8,128)} %class_y_hbm.1, ...), custom_call_target="tpu_custom_call" | custom-call | tf_op jit(solution)/shard_map/pallas_call | solution.py:452
  17.7 1.0 %shard_map.103 = (f32[2,64,512]{2,1,0:T(8,128)}, f32[2,64,512]{2,1,0:T(8,128)}, f32[2,64,512]{2,1,0:T(8,128)}, f32[2,64,512]{2,1,0:T(8,128)}) custom-call(f32[2,64,512]{2,1,0:T(8,128)S(1)} %get-tuple-element.8.refs_0_, f32[2,64,512]{2,1,0:T(8,128)S(1)} %get-tuple-element.9.refs_1_, f32[2,64,512]{2,1,0:T(8,128)S(1)} %get-tuple-element.10.refs_2_, ...), custom_call_target="tpu_custom_call" | custom-call | tf_op jit(solution)/shard_map/pallas_call | solution.py:476

commit v6 on v5

--- a/solution.py
+++ b/solution.py
@@ -9,7 +9,7 @@
 
 F32 = jnp.float32
 PAD = 8
-ROWS = 16
+ROWS = 8
 LANES = 128
 MESSAGES = {
     "cx": {"gx": 1}, "cy": {"gy": 1}, "cv": {"gz": 1},
@@ -203,7 +203,7 @@
     row_send[ROW["vx"]] = volt[:, first, :]
     put_col("vy", volt[:, inner, :LANES], 0)
     pl.semaphore_wait(barrier, group - 1)
-    send("cv", "cx", "cy", "vx", "vy", "vl")
+    send("cx", "cy", "cv", "vx", "vy", "vl")
     receive("cx", "cy", "cv")
 
     cond_x[:, PAD - 1, :] = row_recv[ROW["cx"]]

time: 18.9 us -> 18.9 us (level)
  no operation moved by 1% of the time
where the time goes in v6:
time: 18.9 us; the launch traced here: 18.7 us
  Pallas kernels  18.1 us (96%)
  between operations  0.64 us (3%)
    pallas_call x1, Pallas kernels, body(): pl.pallas_call(functools.partial(kernel, sizes, (lay, nx, ny)), out_shape...  17.1 us
    pallas_call x1, Pallas kernels, body(): pl.pallas_call(write_out, out_shape=(block,) * 4, in_specs=[pl.BlockSpec(...  1 us

profile of v6, /device:TPU:0, one launch (start us, length us, event | category | flops | bytes accessed | tf_op | source)
XLA Modules:
  0.0 18.7 jit_solution(9812848102038670997)
XLA Ops:
  0.6 17.1 %shard_map.102 = (f32[2,64,512]{2,1,0:T(8,128)S(1)}, f32[2,64,512]{2,1,0:T(8,128)S(1)}, f32[2,64,512]{2,1,0:T(8,128)S(1)}, f32[2,64,512]{2,1,0:T(8,128)S(1)}) custom-call(f32[2,64,512]{2,1,0:T(8,128)} %source_hbm.1, f32[2,64,512]{2,1,0:T(8,128)} %volt_hbm.1, s32[2,64,512]{2,1,0:T(8,128)} %class_x_hbm.1, s32[2,64,512]{2,1,0:T(8,128)} %class_y_hbm.1, ...), custom_call_target="tpu_custom_call" | custom-call | tf_op jit(solution)/shard_map/pallas_call | solution.py:452
  17.7 1.0 %shard_map.103 = (f32[2,64,512]{2,1,0:T(8,128)}, f32[2,64,512]{2,1,0:T(8,128)}, f32[2,64,512]{2,1,0:T(8,128)}, f32[2,64,512]{2,1,0:T(8,128)}) custom-call(f32[2,64,512]{2,1,0:T(8,128)S(1)} %get-tuple-element.8.refs_0_, f32[2,64,512]{2,1,0:T(8,128)S(1)} %get-tuple-element.9.refs_1_, f32[2,64,512]{2,1,0:T(8,128)S(1)} %get-tuple-element.10.refs_2_, ...), custom_call_target="tpu_custom_call" | custom-call | tf_op jit(solution)/shard_map/pallas_call | solution.py:476
